TPU v7x, 32 devices: a whole 2x2x4 slice. The times are simulated.
32 devices in a mesh: dp: 8 (over y, x, core), slab: 4 (over z).
Axes of the slice: x: 2, y: 2, z: 4, core: 2. Of those that a mesh axis runs over, the one named last changes fastest.
Arguments:
- features: bfloat16 [8, 8, 16, 16, 256], P('dp', 'slab'), may hold values from -6 to 6
- kernel: bfloat16 [27, 256, 256], replicated, may hold values from -6 to 6
- head_proj: bfloat16 [256, 2], replicated, may hold values from -0.375 to 0.375
- material_ids: int32 [8, 8, 16, 16], P('dp', 'slab'), may hold values from 0 to 3
- port_ids: int32 [8, 8, 16, 16], P('dp', 'slab'), may hold values from 0 to 2
- permittivity: float32 [2, 4], replicated, may hold values from 0.2 to 12
- port_source: float32 [2, 2], replicated, may hold values from -4 to 4
- master: float32 [1769472], P(('dp', 'slab')), may hold values from -0.6 to 0.6
- moment: float32 [1769472], P(('dp', 'slab')), may hold values from -0.06 to 0.06
- second: float32 [1769472], P(('dp', 'slab')), may hold values from 1e-05 to 0.001
Outputs:
- new_master: float32 [1769472], P(('dp', 'slab'))
- new_moment: float32 [1769472], P(('dp', 'slab'))
- new_second: float32 [1769472], P(('dp', 'slab'))
- new_kernel: bfloat16 [27, 256, 256], replicated
All inputs are finite; a program needn't handle non-finite values.
Results may differ from a plain program's by a relative error of at most 0.0034.
Values may be sent and summed in bfloat16 or wider, within the bound.
A program may use at most 64 MiB of HBM per device.

v0:
```python
import jax
import jax.numpy as jnp
from jax import lax
from jax.sharding import PartitionSpec as P

wave_sq = 0.3
beta_one = 0.9
beta_two = 0.99
learn_rate = 0.01
adam_eps = 1e-08


def padded_2(block, sides, width):
    for axis, dim in sides:
        count = lax.axis_size(axis)
        forward = [(i, i + 1) for i in range(count - 1)]
        backward = [(target, source) for source, target in forward]
        low = lax.ppermute(
            lax.slice_in_dim(block, block.shape[dim] - width, None, axis=dim), axis, forward
        )
        high = lax.ppermute(lax.slice_in_dim(block, 0, width, axis=dim), axis, backward)
        block = jnp.concatenate([low, block, high], axis=dim)
    return block


def laplace(extended):
    padded = jnp.pad(extended, ((0, 0), (1, 1), (1, 1), (0, 0)))
    centre = padded[1:-1, 1:-1, 1:-1]
    near = padded[2:, 1:-1, 1:-1] + padded[:-2, 1:-1, 1:-1]
    near = near + padded[1:-1, 2:, 1:-1] + padded[1:-1, :-2, 1:-1]
    near = near + padded[1:-1, 1:-1, 2:] + padded[1:-1, 1:-1, :-2]
    return near - 6.0 * centre


def lookup(codes, table, offset):
    count = table.shape[1]
    values = jnp.arange(count, dtype=jnp.int32) + offset
    hits = codes[..., None] == values
    real_part = jnp.sum(jnp.where(hits, table[0], 0.0), axis=-1)
    imag_part = jnp.sum(jnp.where(hits, table[1], 0.0), axis=-1)
    return (real_part, imag_part)


def body(
    features,
    kernel,
    head_proj,
    material_ids,
    port_ids,
    permittivity,
    port_source,
    master,
    moment,
    second,
):
    feats = features[0]
    slab_depth, grid_rows, grid_cols, channels = feats.shape
    cell_count = slab_depth * grid_rows * grid_cols
    all_cells = cell_count * lax.axis_size("dp") * lax.axis_size("slab")
    weight_scale = 1.0 / jnp.sqrt(jnp.float32(27 * channels))
    with_rim = padded_2(features, (("slab", 1),), 1)[0]
    padded = jnp.pad(with_rim, ((0, 0), (1, 1), (1, 1), (0, 0)))
    pieces = []
    summed = jnp.zeros((cell_count, channels), jnp.float32)
    for tap_index in range(27):
        shift_z, shift_y, shift_x = (tap_index // 9, tap_index // 3 % 3, tap_index % 3)
        partial_rows = padded[
            shift_z : shift_z + slab_depth,
            shift_y : shift_y + grid_rows,
            shift_x : shift_x + grid_cols,
        ].reshape(cell_count, channels)
        pieces.append(partial_rows)
        summed = summed + jnp.dot(
            partial_rows, kernel[tap_index], preferred_element_type=jnp.float32
        )
    preact = summed * weight_scale
    hidden = jax.nn.silu(preact).astype(jnp.bfloat16)
    field_vals = jnp.dot(hidden, head_proj, preferred_element_type=jnp.float32).reshape(
        slab_depth, grid_rows, grid_cols, 2
    )
    eps_re, eps_im = lookup(material_ids[0], permittivity, 0)
    src_re, src_im = lookup(port_ids[0], port_source, 1)
    field_ext = padded_2(field_vals, (("slab", 0),), 1)
    lap_field = laplace(field_ext)
    field_re, field_im = (field_vals[..., 0], field_vals[..., 1])
    res_re = lap_field[..., 0] + wave_sq * (eps_re * field_re - eps_im * field_im) - src_re
    res_im = lap_field[..., 1] + wave_sq * (eps_re * field_im + eps_im * field_re) - src_im
    norm_scale = 2.0 / jnp.sqrt(jnp.float32(all_cells))
    adjoint = jnp.stack([res_re * norm_scale, res_im * norm_scale], axis=-1)
    adj_ext = padded_2(adjoint, (("slab", 0),), 1)
    lap_adj = laplace(adj_ext)
    grad_re = lap_adj[..., 0] + wave_sq * (eps_re * adjoint[..., 0] + eps_im * adjoint[..., 1])
    grad_im = lap_adj[..., 1] + wave_sq * (eps_re * adjoint[..., 1] - eps_im * adjoint[..., 0])
    grad_field = jnp.stack([grad_re, grad_im], axis=-1).reshape(cell_count, 2)
    d_hidden = jnp.dot(grad_field, head_proj.astype(jnp.float32).T, precision=lax.Precision.HIGHEST)
    sigma = jax.nn.sigmoid(preact)
    d_pre = (d_hidden * sigma * (1.0 + preact * (1.0 - sigma))).astype(jnp.bfloat16)
    grads = []
    for tap_index in range(27):
        grads.append(
            lax.dot_general(
                pieces[tap_index],
                d_pre,
                (((0,), (0,)), ((), ())),
                preferred_element_type=jnp.float32,
            )
        )
    flat_grad = (jnp.stack(grads, axis=0) * weight_scale).reshape(-1)
    grad_share = lax.psum_scatter(flat_grad, ("dp", "slab"), scatter_dimension=0, tiled=True)
    new_moment = beta_one * moment + (1.0 - beta_one) * grad_share
    new_second = beta_two * second + (1.0 - beta_two) * grad_share * grad_share
    new_master = master - learn_rate * new_moment / (jnp.sqrt(new_second) + adam_eps)
    rounded = new_master.astype(jnp.bfloat16)
    gathered = lax.all_gather(rounded, ("dp", "slab"), axis=0, tiled=True)
    new_kernel = gathered.reshape(kernel.shape)
    return (new_master, new_moment, new_second, new_kernel)


def solution(mesh):
    placed = (
        P("dp", "slab", None, None, None),
        P(),
        P(),
        P("dp", "slab", None, None),
        P("dp", "slab", None, None),
        P(),
        P(),
        P(("dp", "slab")),
        P(("dp", "slab")),
        P(("dp", "slab")),
    )
    return jax.shard_map(
        body,
        mesh=mesh,
        in_specs=placed,
        out_specs=(P(("dp", "slab")), P(("dp", "slab")), P(("dp", "slab")), P()),
        check_vma=False,
    )
```

profile of v0, /device:TPU:21, one launch (start us, length us, event | category | flops | bytes accessed | tf_op | source)
XLA Modules:
  0.0 313.5 jit_solution(14361041598451991147)
XLA Ops:
  7.2 1.1 fusion.122
  8.4 3.3 %collective-permute-start = (bf16[1,1,16,16,256]{4,3,2,1,0:T(8,128)(2,1)S(1)}, bf16[1,1,16,16,256]{4,3,2,1,0:T(8,128)(2,1)S(1)}, u32[]{:S(2)}, u32[]{:S(2)}) collective-permute-start(bf16[1,1,16,16,256]{4,3,2,1,0:T(8,128)(2,1)S(1)} %get-tuple-element.38), channel_id=1, source_target_pairs={{0,1},{1,2},{2,3},{4,5},{5,6},{6,7},{8,9},{9,10},{10,11},{12,13},{... | collective-permute-start | bytes 393224 | tf_op jit(solution)/shard_map/ppermute | solution.py:18
  11.7 2.1 collective-permute-start.1
  13.8 0.8 slice_bitcast_fusion.2
  14.6 0.8 slice_bitcast_fusion
  15.3 0.8 select_reduce_fusion.1
  16.1 1.3 collective-permute-done.1
  17.4 1.0 maximum_bitcast_fusion
  18.5 0.6 pad_slice_fusion
  19.2 0.3 pad_slice_fusion.1
  26.1 0.8 copy-done.28
  27.1 0.7 slice.326
  27.8 2.1 collective-permute-start.2
  29.9 0.7 slice.329
  30.6 3.2 %collective-permute-start.3 = (f32[1,16,16,2]{2,1,0,3:T(8,128)}, f32[1,16,16,2]{2,1,0,3:T(8,128)S(1)}, u32[]{:S(2)}, u32[]{:S(2)}) collective-permute-start(f32[1,16,16,2]{2,1,0,3:T(8,128)} %bitcast.56), channel_id=1, source_target_pairs={{0,1},{1,2},{2,3},{4,5},{5,6},{6,7},{8,9},{9,10},{10,11},{12,13},{... | collective-permute-start | bytes 6152 | tf_op jit(solution)/shard_map/ppermute | solution.py:18
  33.9 1.4 collective-permute-done.3
  35.6 2.1 collective-permute-start.4
  37.7 3.4 %collective-permute-start.5 = (f32[1,16,16,2]{2,1,0,3:T(8,128)S(1)}, f32[1,16,16,2]{2,1,0,3:T(8,128)S(1)}, u32[]{:S(2)}, u32[]{:S(2)}) collective-permute-start(f32[1,16,16,2]{2,1,0,3:T(8,128)S(1)} %get-tuple-element.44), channel_id=1, source_target_pairs={{0,1},{1,2},{2,3},{4,5},{5,6},{6,7},{8,9},{9,10},{10,11},{12,13},{... | collective-permute-start | bytes 6152 | tf_op jit(solution)/shard_map/ppermute | solution.py:18
  41.1 1.1 collective-permute-done.5
  42.6 1.7 fusion.4
  44.3 0.3 fusion.31
  44.6 1.2 fusion.30
  45.8 1.2 fusion.29
  47.1 1.2 fusion.28
  48.3 0.3 fusion.27
  48.6 0.3 fusion.26
  48.9 0.3 fusion.25
  49.1 0.3 fusion.24
  49.7 0.3 fusion.22
  50.0 0.3 fusion.21
  50.9 0.3 fusion.18
  51.2 0.3 fusion.17
  52.0 0.3 fusion.14
  52.3 0.3 fusion.13
  52.6 0.3 fusion.12
  52.9 0.3 fusion.11
  53.1 0.3 fusion.10
  53.4 0.3 fusion.9
  53.7 0.3 fusion.8
  54.0 0.3 fusion.7
  54.3 0.3 fusion.6
  54.5 0.3 fusion.5
  54.8 3.5 %broadcast_multiply_fusion = f32[27,256,256]{2,1,0:T(8,128)} fusion(f32[27,256,256]{2,1,0:T(8,128)S(1)} %fusion.5), kind=kLoop, calls=%fused_computation | loop fusion | flops 1769472 | bytes 14155776 | tf_op jit(solution)/shard_map/mul | solution.py:108
  58.4 9.5 %copy.28 = f32[864,2,8,128]{3,1,2,0:T(2,128)} copy(f32[864,2,8,128]{3,2,1,0:T(8,128)} %bitcast.378) | data formatting | bytes 14155776
  68.0 169.0 %all-reduce.6.cloned.1.call-done = f32[1769472]{0:T(1024)} async-done(((f32[1769472]{0:T(1024)}), f32[1769472]{0:T(1024)}) %all-reduce.6.cloned.1.call-update) | async-done | bytes 7077904
  237.0 1.9 fusion.120
  238.9 61.3 %all-gather.2.cloned.1.call-done = bf16[1769472]{0:T(1024)(128)(2,1)} async-done(((bf16[55296]{0:T(1024)(128)(2,1)}), bf16[1769472]{0:T(1024)(128)(2,1)}) %all-gather.2.cloned.1.call-update) | async-done | bytes 3538960 | tf_op jit(solution)/shard_map/all_gather | solution.py:114
  300.2 6.4 %reshape.158 = bf16[27,256,256]{2,1,0:T(8,128)(2,1)} reshape(bf16[1769472]{0:T(1024)(128)(2,1)} %all-gather.2.cloned.1.call-done) | data formatting | bytes 7077888 | tf_op jit(solution)/shard_map/reshape | solution.py:115
  (119 shorter events, 8.8 us)
Async XLA Ops:
  7.2 19.7 %copy-start = (bf16[256,2]{0,1:T(2,128)(2,1)S(1)}, bf16[256,2]{0,1:T(2,128)(2,1)}, u32[]{:S(2)}) copy-start(bf16[256,2]{0,1:T(2,128)(2,1)} %param.12) | copy-start | bytes 3076
  7.2 229.8 %all-reduce.6.cloned.1.call-start = ((), (), s32[]{:S(2)}) async-start(), calls=%async_computation.1 | async-start | bytes 14155776
  7.2 12.3 %copy-start.2 = (bf16[27,256,256]{2,1,0:T(8,128)(2,1)S(1)}, bf16[27,256,256]{2,1,0:T(8,128)(2,1)}, u32[]{:S(2)}) copy-start(bf16[27,256,256]{2,1,0:T(8,128)(2,1)} %param.11) | copy-start | bytes 10616836
  8.4 7.8 %collective-permute-start = (bf16[1,1,16,16,256]{4,3,2,1,0:T(8,128)(2,1)S(1)}, bf16[1,1,16,16,256]{4,3,2,1,0:T(8,128)(2,1)S(1)}, u32[]{:S(2)}, u32[]{:S(2)}) collective-permute-start(bf16[1,1,16,16,256]{4,3,2,1,0:T(8,128)(2,1)S(1)} %get-tuple-element.38), channel_id=1, source_target_pairs={{0,1},{1,2},{2,3},{4,5},{5,6},{6,7},{8,9},{9,10},{10,11},{12,13},{... | collective-permute-start | bytes 393224 | tf_op jit(solution)/shard_map/ppermute | solution.py:18
  11.7 5.7 %collective-permute-start.1 = (bf16[1,1,16,16,256]{4,3,2,1,0:T(8,128)(2,1)S(1)}, bf16[1,1,16,16,256]{4,3,2,1,0:T(8,128)(2,1)S(1)}, u32[]{:S(2)}, u32[]{:S(2)}) collective-permute-start(bf16[1,1,16,16,256]{4,3,2,1,0:T(8,128)(2,1)S(1)} %get-tuple-element.39), channel_id=1, source_target_pairs={{1,0},{2,1},{3,2},{5,4},{6,5},{7,6},{9,8},{10,9},{11,10},{13,12},{... | collective-permute-start | bytes 393224 | tf_op jit(solution)/shard_map/ppermute | solution.py:21
  18.4 2.5 copy-start.1
  19.1 1.6 copy-start.25
  19.1 2.6 copy-start.21
  19.1 2.6 copy-start.23
  19.1 2.6 copy-start.26
  19.1 2.6 copy-start.27
  19.1 2.6 copy-start.19
  19.2 2.9 copy-start.17
  19.2 3.1 copy-start.15
  19.2 3.3 %copy-start.13 = (bf16[2,16,16,256]{3,2,1,0:T(8,128)(2,1)}, bf16[2,16,16,256]{3,2,1,0:T(8,128)(2,1)S(1)}, u32[]{:S(2)}) copy-start(bf16[2,16,16,256]{3,2,1,0:T(8,128)(2,1)S(1)} %get-tuple-element.22) | copy-start | bytes 786436
  19.2 3.5 %copy-start.11 = (bf16[2,16,16,256]{3,2,1,0:T(8,128)(2,1)}, bf16[2,16,16,256]{3,2,1,0:T(8,128)(2,1)S(1)}, u32[]{:S(2)}) copy-start(bf16[2,16,16,256]{3,2,1,0:T(8,128)(2,1)S(1)} %get-tuple-element.23) | copy-start | bytes 786436
  19.2 4.0 %copy-start.9 = (bf16[2,16,16,256]{3,2,1,0:T(8,128)(2,1)}, bf16[2,16,16,256]{3,2,1,0:T(8,128)(2,1)S(1)}, u32[]{:S(2)}) copy-start(bf16[2,16,16,256]{3,2,1,0:T(8,128)(2,1)S(1)} %get-tuple-element.24) | copy-start | bytes 786436
  19.2 4.2 %copy-start.7 = (bf16[2,16,16,256]{3,2,1,0:T(8,128)(2,1)}, bf16[2,16,16,256]{3,2,1,0:T(8,128)(2,1)S(1)}, u32[]{:S(2)}) copy-start(bf16[2,16,16,256]{3,2,1,0:T(8,128)(2,1)S(1)} %get-tuple-element.25) | copy-start | bytes 786436
  19.2 4.5 %copy-start.5 = (bf16[2,16,16,256]{3,2,1,0:T(8,128)(2,1)}, bf16[2,16,16,256]{3,2,1,0:T(8,128)(2,1)S(1)}, u32[]{:S(2)}) copy-start(bf16[2,16,16,256]{3,2,1,0:T(8,128)(2,1)S(1)} %get-tuple-element.26) | copy-start | bytes 786436
  19.2 4.7 %copy-start.3 = (bf16[2,16,16,256]{3,2,1,0:T(8,128)(2,1)}, bf16[2,16,16,256]{3,2,1,0:T(8,128)(2,1)S(1)}, u32[]{:S(2)}) copy-start(bf16[2,16,16,256]{3,2,1,0:T(8,128)(2,1)S(1)} %get-tuple-element.27) | copy-start | bytes 786436
  24.2 9.6 %copy-start.32 = (s32[1,2,16,16]{3,2,1,0:T(8,128)S(1)}, s32[1,2,16,16]{3,2,1,0:T(8,128)}, u32[]{:S(2)}) copy-start(s32[1,2,16,16]{3,2,1,0:T(8,128)} %param.14) | copy-start | bytes 6148
  26.0 0.8 copy-start.28
  27.8 6.1 %collective-permute-start.2 = (f32[1,16,16,2]{2,1,0,3:T(8,128)}, f32[1,16,16,2]{2,1,0,3:T(8,128)S(1)}, u32[]{:S(2)}, u32[]{:S(2)}) collective-permute-start(f32[1,16,16,2]{2,1,0,3:T(8,128)} %bitcast.55), channel_id=1, source_target_pairs={{1,0},{2,1},{3,2},{5,4},{6,5},{7,6},{9,8},{10,9},{11,10},{13,12},{... | collective-permute-start | bytes 6152 | tf_op jit(solution)/shard_map/ppermute | solution.py:21
  30.6 4.8 %collective-permute-start.3 = (f32[1,16,16,2]{2,1,0,3:T(8,128)}, f32[1,16,16,2]{2,1,0,3:T(8,128)S(1)}, u32[]{:S(2)}, u32[]{:S(2)}) collective-permute-start(f32[1,16,16,2]{2,1,0,3:T(8,128)} %bitcast.56), channel_id=1, source_target_pairs={{0,1},{1,2},{2,3},{4,5},{5,6},{6,7},{8,9},{9,10},{10,11},{12,13},{... | collective-permute-start | bytes 6152 | tf_op jit(solution)/shard_map/ppermute | solution.py:18
  35.6 5.5 %collective-permute-start.4 = (f32[1,16,16,2]{2,1,0,3:T(8,128)S(1)}, f32[1,16,16,2]{2,1,0,3:T(8,128)S(1)}, u32[]{:S(2)}, u32[]{:S(2)}) collective-permute-start(f32[1,16,16,2]{2,1,0,3:T(8,128)S(1)} %get-tuple-element.45), channel_id=1, source_target_pairs={{1,0},{2,1},{3,2},{5,4},{6,5},{7,6},{9,8},{10,9},{11,10},{13,12},{... | collective-permute-start | bytes 6152 | tf_op jit(solution)/shard_map/ppermute | solution.py:21
  37.7 4.5 %collective-permute-start.5 = (f32[1,16,16,2]{2,1,0,3:T(8,128)S(1)}, f32[1,16,16,2]{2,1,0,3:T(8,128)S(1)}, u32[]{:S(2)}, u32[]{:S(2)}) collective-permute-start(f32[1,16,16,2]{2,1,0,3:T(8,128)S(1)} %get-tuple-element.44), channel_id=1, source_target_pairs={{0,1},{1,2},{2,3},{4,5},{5,6},{6,7},{8,9},{9,10},{10,11},{12,13},{... | collective-permute-start | bytes 6152 | tf_op jit(solution)/shard_map/ppermute | solution.py:18
  42.5 6.3 %copy-start.24 = (bf16[2,16,16,256]{3,2,1,0:T(8,128)(2,1)S(1)}, bf16[2,16,16,256]{3,2,1,0:T(8,128)(2,1)}, u32[]{:S(2)}) copy-start(bf16[2,16,16,256]{3,2,1,0:T(8,128)(2,1)} %copy-done.23) | copy-start | bytes 786436
  42.5 6.6 %copy-start.22 = (bf16[2,16,16,256]{3,2,1,0:T(8,128)(2,1)S(1)}, bf16[2,16,16,256]{3,2,1,0:T(8,128)(2,1)}, u32[]{:S(2)}) copy-start(bf16[2,16,16,256]{3,2,1,0:T(8,128)(2,1)} %copy-done.21) | copy-start | bytes 786436
  42.5 6.9 %copy-start.20 = (bf16[2,16,16,256]{3,2,1,0:T(8,128)(2,1)S(1)}, bf16[2,16,16,256]{3,2,1,0:T(8,128)(2,1)}, u32[]{:S(2)}) copy-start(bf16[2,16,16,256]{3,2,1,0:T(8,128)(2,1)} %copy-done.19) | copy-start | bytes 786436
  42.6 7.2 %copy-start.18 = (bf16[2,16,16,256]{3,2,1,0:T(8,128)(2,1)S(1)}, bf16[2,16,16,256]{3,2,1,0:T(8,128)(2,1)}, u32[]{:S(2)}) copy-start(bf16[2,16,16,256]{3,2,1,0:T(8,128)(2,1)} %copy-done.17) | copy-start | bytes 786436
  42.6 7.4 %copy-start.16 = (bf16[2,16,16,256]{3,2,1,0:T(8,128)(2,1)S(1)}, bf16[2,16,16,256]{3,2,1,0:T(8,128)(2,1)}, u32[]{:S(2)}) copy-start(bf16[2,16,16,256]{3,2,1,0:T(8,128)(2,1)} %copy-done.15) | copy-start | bytes 786436
  42.6 7.7 %copy-start.14 = (bf16[2,16,16,256]{3,2,1,0:T(8,128)(2,1)S(1)}, bf16[2,16,16,256]{3,2,1,0:T(8,128)(2,1)}, u32[]{:S(2)}) copy-start(bf16[2,16,16,256]{3,2,1,0:T(8,128)(2,1)} %copy-done.13) | copy-start | bytes 786436
  42.6 8.0 %copy-start.12 = (bf16[2,16,16,256]{3,2,1,0:T(8,128)(2,1)S(1)}, bf16[2,16,16,256]{3,2,1,0:T(8,128)(2,1)}, u32[]{:S(2)}) copy-start(bf16[2,16,16,256]{3,2,1,0:T(8,128)(2,1)} %copy-done.11) | copy-start | bytes 786436
  42.6 8.6 %copy-start.10 = (bf16[2,16,16,256]{3,2,1,0:T(8,128)(2,1)S(1)}, bf16[2,16,16,256]{3,2,1,0:T(8,128)(2,1)}, u32[]{:S(2)}) copy-start(bf16[2,16,16,256]{3,2,1,0:T(8,128)(2,1)} %copy-done.9) | copy-start | bytes 786436
  42.6 8.8 %copy-start.8 = (bf16[2,16,16,256]{3,2,1,0:T(8,128)(2,1)S(1)}, bf16[2,16,16,256]{3,2,1,0:T(8,128)(2,1)}, u32[]{:S(2)}) copy-start(bf16[2,16,16,256]{3,2,1,0:T(8,128)(2,1)} %copy-done.7) | copy-start | bytes 786436
  42.6 9.1 %copy-start.6 = (bf16[2,16,16,256]{3,2,1,0:T(8,128)(2,1)S(1)}, bf16[2,16,16,256]{3,2,1,0:T(8,128)(2,1)}, u32[]{:S(2)}) copy-start(bf16[2,16,16,256]{3,2,1,0:T(8,128)(2,1)} %copy-done.5) | copy-start | bytes 786436
  44.3 7.7 %copy-start.4 = (bf16[2,16,16,256]{3,2,1,0:T(8,128)(2,1)S(1)}, bf16[2,16,16,256]{3,2,1,0:T(8,128)(2,1)}, u32[]{:S(2)}) copy-start(bf16[2,16,16,256]{3,2,1,0:T(8,128)(2,1)} %copy-done.3) | copy-start | bytes 786436
  67.9 169.1 %copy-start.29 = (f32[55296]{0:T(1024)S(1)}, f32[55296]{0:T(1024)}, u32[]{:S(2)}) copy-start(f32[55296]{0:T(1024)} %param.17) | copy-start | bytes 663556
  67.9 169.1 %copy-start.30 = (f32[55296]{0:T(1024)S(1)}, f32[55296]{0:T(1024)}, u32[]{:S(2)}) copy-start(f32[55296]{0:T(1024)} %param.18) | copy-start | bytes 663556
  67.9 169.1 %copy-start.31 = (f32[55296]{0:T(1024)S(1)}, f32[55296]{0:T(1024)}, u32[]{:S(2)}) copy-start(f32[55296]{0:T(1024)} %param.19) | copy-start | bytes 663556
  67.9 232.3 %all-gather.2.cloned.1.call-start = ((), (), s32[]{:S(2)}) async-start(), calls=%async_computation | async-start | bytes 3649536 | tf_op jit(solution)/shard_map/all_gather | solution.py:114
Sparse Core Ops, SparseCore 0:
  68.0 168.9 all-reduce.5
  240.8 59.4 all-gather.1
where the time goes:
time: 317 us; the launch traced here: 313 us
  waiting for transfers between devices  234 us (74%)
  local copies, waits for them, and re-layouts  22 us (7%)
  matrix products  18.2 us (6%)
  starting transfers between devices  16.2 us (5%)
  between operations  15 us (5%)
  other arithmetic  7.79 us (2%)
    unnamed x3, waiting for transfers between devices  169 us
    all_gather x1, waiting for transfers between devices, body(): gathered = lax.all_gather(rounded, ('dp', 'slab'), axis=0, tiled=True)  61.3 us
    unnamed x67, local copies, waits for them, and re-layouts  10.4 us
    dot_general x27, matrix products, body(): lax.dot_general(pieces[tap_index], d_pre, (((0,), (0,)), ((), ())), prefe...  10.2 us
    ppermute x3, starting transfers between devices, padded_2(): lax.ppermute(lax.slice_in_dim(block, block.shape[dim] - width, None, axis...  9.92 us
    reshape x1, local copies, waits for them, and re-layouts, body(): new_kernel = gathered.reshape(kernel.shape)  6.4 us
  transfers between devices with their start and end apart: 8, of which 5 were waited for; matrix products, arithmetic and copies ran while one was open for 1% of the time, Pallas kernels for 0%

commit v1 on v0

--- a/solution.py
+++ b/solution.py
@@ -1,6 +1,11 @@
+import functools
+
 import jax
 import jax.numpy as jnp
+import numpy as np
 from jax import lax
+from jax.experimental import pallas as pl
+from jax.experimental.pallas import tpu as pltpu
 from jax.sharding import PartitionSpec as P
 
 wave_sq = 0.3
@@ -39,6 +44,237 @@
     real_part = jnp.sum(jnp.where(hits, table[0], 0.0), axis=-1)
     imag_part = jnp.sum(jnp.where(hits, table[1], 0.0), axis=-1)
     return (real_part, imag_part)
+
+
+def widen(block, rows):
+    extra = rows - block.shape[0]
+    if extra:
+        block = jnp.concatenate([block, jnp.zeros((extra, block.shape[1]), block.dtype)], axis=0)
+    return block.astype(jnp.bfloat16)
+
+
+def share_kernel(
+    scale,
+    grad,
+    master,
+    moment,
+    second,
+    new_master,
+    new_moment,
+    new_second,
+    full,
+    pair_in,
+    group_out,
+    group_in,
+    line_out,
+    line_in,
+    narrow,
+    pair_send,
+    pair_recv,
+    group_send,
+    group_recv,
+    line_send,
+    line_recv,
+    line_back_send,
+    line_back_recv,
+    group_back_send,
+    group_back_recv,
+    pair_back_send,
+    pair_back_recv,
+):
+    groups, _, line, rows, width = grad.shape
+    padded = full.shape[3]
+    dp = lax.axis_index("dp")
+    here = lax.axis_index("slab")
+    mine = dp // 2
+    core = dp % 2
+    sibling = (mine * 2 + 1 - core, here)
+
+    def group_at(step):
+        return (mine + step + groups) % groups
+
+    def slab_at(step):
+        return (here + step + line) % line
+
+    def group_device(step):
+        return (group_at(step) * 2 + core, here)
+
+    def line_device(step):
+        return (dp, slab_at(step))
+
+    def remote(source, target, send, recv, device):
+        return pltpu.make_async_remote_copy(
+            src_ref=source,
+            dst_ref=target,
+            send_sem=send,
+            recv_sem=recv,
+            device_id=device,
+            device_id_type=pl.DeviceIdType.MESH,
+        )
+
+    def pair_copy(k):
+        return remote(
+            grad.at[group_at(k), 1 - core], pair_in.at[k], pair_send.at[k], pair_recv.at[k], sibling
+        )
+
+    def group_copy(k, j):
+        return remote(
+            group_out.at[k - 1, j],
+            group_in.at[k - 1, j],
+            group_send.at[k - 1, j],
+            group_recv.at[k - 1, j],
+            group_device(k),
+        )
+
+    def line_copy(j):
+        return remote(
+            line_out.at[j - 1], line_in.at[j - 1], line_send.at[j - 1], line_recv.at[j - 1], line_device(j)
+        )
+
+    def line_back(j):
+        spot = full.at[mine, core, here]
+        return remote(spot, spot, line_back_send.at[j - 1], line_back_recv.at[j - 1], line_device(j))
+
+    def group_back(k, j):
+        spot = full.at[mine, core, slab_at(-j)]
+        return remote(
+            spot, spot, group_back_send.at[k - 1, j], group_back_recv.at[k - 1, j], group_device(k)
+        )
+
+    def pair_back(k, j):
+        spot = full.at[group_at(-k), core, slab_at(-j)]
+        return remote(spot, spot, pair_back_send.at[k, j], pair_back_recv.at[k, j], sibling)
+
+    others = [sibling]
+    others += [group_device(k) for k in range(1, groups)]
+    others += [line_device(j) for j in range(1, line)]
+    barrier = pltpu.get_barrier_semaphore()
+    for device in others:
+        pl.semaphore_signal(barrier, inc=1, device_id=device, device_id_type=pl.DeviceIdType.MESH)
+    pl.semaphore_wait(barrier, len(others))
+
+    group_order = list(range(1, groups)) + [0]
+    line_order = list(range(1, line)) + [0]
+    for k in group_order:
+        pair_copy(k).start()
+    for k in group_order[:-1]:
+        pair_copy(k).wait_recv()
+        for j in line_order:
+            slab = slab_at(j)
+            group_out[k - 1, j] = widen(grad[group_at(k), core, slab] + pair_in[k, slab], padded)
+            group_copy(k, j).start()
+    pair_copy(0).wait_recv()
+    total = None
+    for j in line_order:
+        slab = slab_at(j)
+        total = grad[mine, core, slab] + pair_in[0, slab]
+        for k in range(1, groups):
+            group_copy(k, j).wait_recv()
+            total = total + group_in[k - 1, j].astype(jnp.float32)[:rows]
+        if j:
+            line_out[j - 1] = widen(total, padded)
+            line_copy(j).start()
+    for j in range(1, line):
+        line_copy(j).wait_recv()
+        total = total + line_in[j - 1].astype(jnp.float32)[:rows]
+
+    total = total * scale
+    parts = width // 128
+    for part in range(parts):
+        narrow[pl.ds(part, rows, stride=parts), :] = total[:, part * 128 : part * 128 + 128]
+    share = narrow[...]
+    stepped = beta_one * moment[...] + (1.0 - beta_one) * share
+    squared = beta_two * second[...] + (1.0 - beta_two) * share * share
+    updated = master[...] - learn_rate * stepped / (jnp.sqrt(squared) + adam_eps)
+    new_moment[...] = stepped
+    new_second[...] = squared
+    new_master[...] = updated
+    narrow[...] = updated
+    block = jnp.concatenate(
+        [narrow[pl.ds(part, rows, stride=parts), :] for part in range(parts)], axis=1
+    )
+    full[mine, core, here] = widen(block, padded)
+
+    for j in range(1, line):
+        line_back(j).start()
+    for k in range(1, groups):
+        group_back(k, 0).start()
+    pair_back(0, 0).start()
+    for j in range(1, line):
+        line_back(j).wait_recv()
+        for k in range(1, groups):
+            group_back(k, j).start()
+        pair_back(0, j).start()
+    for j in range(line):
+        for k in range(1, groups):
+            group_back(k, j).wait_recv()
+            pair_back(k, j).start()
+    for j in range(line):
+        for k in range(groups):
+            pair_back(k, j).wait_recv()
+    for k in range(groups):
+        pair_copy(k).wait_send()
+        for j in range(line):
+            pair_back(k, j).wait_send()
+            if k:
+                group_copy(k, j).wait_send()
+                group_back(k, j).wait_send()
+    for j in range(1, line):
+        line_copy(j).wait_send()
+        line_back(j).wait_send()
+
+
+def share_and_step(grad, master, moment, second, scale):
+    rows_all, width = grad.shape
+    groups = lax.axis_size("dp") // 2
+    line = lax.axis_size("slab")
+    rows = rows_all // (groups * 2 * line)
+    padded = -(-rows // 16) * 16
+    flat = (master.size // 128, 128)
+    vmem = pl.BlockSpec(memory_space=pltpu.VMEM)
+    dma = pltpu.SemaphoreType.DMA
+    state = jax.ShapeDtypeStruct(flat, jnp.float32)
+    out = pl.pallas_call(
+        functools.partial(share_kernel, scale),
+        out_shape=[
+            state,
+            state,
+            state,
+            jax.ShapeDtypeStruct((groups, 2, line, padded, width), jnp.bfloat16),
+        ],
+        in_specs=[vmem] * 4,
+        out_specs=[vmem] * 4,
+        scratch_shapes=[
+            pltpu.VMEM((groups, line, rows, width), jnp.float32),
+            pltpu.VMEM((groups - 1, line, padded, width), jnp.bfloat16),
+            pltpu.VMEM((groups - 1, line, padded, width), jnp.bfloat16),
+            pltpu.VMEM((line - 1, padded, width), jnp.bfloat16),
+            pltpu.VMEM((line - 1, padded, width), jnp.bfloat16),
+            pltpu.VMEM(flat, jnp.float32),
+            dma((groups,)),
+            dma((groups,)),
+            dma((groups - 1, line)),
+            dma((groups - 1, line)),
+            dma((line - 1,)),
+            dma((line - 1,)),
+            dma((line - 1,)),
+            dma((line - 1,)),
+            dma((groups - 1, line)),
+            dma((groups - 1, line)),
+            dma((groups, line)),
+            dma((groups, line)),
+        ],
+        compiler_params=pltpu.CompilerParams(
+            collective_id=0, has_side_effects=True, vmem_limit_bytes=48 * 1024 * 1024
+        ),
+    )(
+        grad.reshape(groups, 2, line, rows, width),
+        master.reshape(flat),
+        moment.reshape(flat),
+        second.reshape(flat),
+    )
+    full = out[3][:, :, :, :rows].reshape(rows_all, width)
+    return [part.reshape(-1) for part in out[:3]] + [full]
 
 
 def body(
@@ -105,14 +341,10 @@
                 preferred_element_type=jnp.float32,
             )
         )
-    flat_grad = (jnp.stack(grads, axis=0) * weight_scale).reshape(-1)
-    grad_share = lax.psum_scatter(flat_grad, ("dp", "slab"), scatter_dimension=0, tiled=True)
-    new_moment = beta_one * moment + (1.0 - beta_one) * grad_share
-    new_second = beta_two * second + (1.0 - beta_two) * grad_share * grad_share
-    new_master = master - learn_rate * new_moment / (jnp.sqrt(new_second) + adam_eps)
-    rounded = new_master.astype(jnp.bfloat16)
-    gathered = lax.all_gather(rounded, ("dp", "slab"), axis=0, tiled=True)
-    new_kernel = gathered.reshape(kernel.shape)
+    grad = jnp.concatenate(grads, axis=0)
+    scale = float(np.float32(1.0) / np.sqrt(np.float32(27 * channels)))
+    new_master, new_moment, new_second, full = share_and_step(grad, master, moment, second, scale)
+    new_kernel = full.reshape(kernel.shape)
     return (new_master, new_moment, new_second, new_kernel)
 
 

time: 317 us -> 121 us (0.38)
  waiting for transfers between devices: 234 us -> 4.81 us
  Pallas kernels: 0 us -> 64.2 us
  between operations: 15 us -> 1.67 us
  local copies, waits for them, and re-layouts: 22 us -> 13.2 us
  other arithmetic: 7.79 us -> 2.36 us
    unnamed x3 -> x0, waiting for transfers between devices: 169 us -> none
    pallas_call x0 -> x1, Pallas kernels: none -> 64.2 us  [share_and_step(): pl.pallas_call(functools.partial(share_kernel, scale), out_shape=[state,...]
    all_gather x1 -> x0, waiting for transfers between devices: 61.3 us -> none  [body(): gathered = lax.all_gather(rounded, ('dp', 'slab'), axis=0, tiled=True)]
    reshape x1 -> x0, local copies, waits for them, and re-layouts: 6.4 us -> none  [body(): new_kernel = gathered.reshape(kernel.shape)]
    unnamed x67 -> x71, local copies, waits for them, and re-layouts: 10.4 us -> 5.88 us
    mul x1 -> x0, other arithmetic: 3.54 us -> none  [body(): flat_grad = (jnp.stack(grads, axis=0) * weight_scale).reshape(-1)]
  transfers between devices with their start and end apart: 8 -> 6, of which waited for: 5 -> 3; matrix products, arithmetic and copies ran while one was open for 1% -> 2% of each run, Pallas kernels for 0% -> 0%
where the time goes in v1:
time: 121 us; the launch traced here: 120 us
  Pallas kernels  64.2 us (53%)
  matrix products  18.2 us (15%)
  starting transfers between devices  16.1 us (13%)
  local copies, waits for them, and re-layouts  13.2 us (11%)
  waiting for transfers between devices  4.81 us (4%)
  other arithmetic  2.36 us (2%)
  between operations  1.67 us (1%)
    pallas_call x1, Pallas kernels, share_and_step(): pl.pallas_call(functools.partial(share_kernel, scale), out_shape=[state,...  64.2 us
    dot_general x27, matrix products, body(): lax.dot_general(pieces[tap_index], d_pre, (((0,), (0,)), ((), ())), prefe...  10.2 us
    ppermute x3, starting transfers between devices, padded_2(): lax.ppermute(lax.slice_in_dim(block, block.shape[dim] - width, None, axis...  9.74 us
    ppermute x3, starting transfers between devices, padded_2(): lax.ppermute(lax.slice_in_dim(block, 0, width, axis=dim), axis, backward)  6.4 us
    dot_general x27, matrix products, body(): jnp.dot(partial_rows, kernel[tap_index], preferred_element_type=jnp.float32)  6.07 us
    unnamed x71, local copies, waits for them, and re-layouts  5.88 us
    ppermute x3, waiting for transfers between devices, padded_2(): lax.ppermute(lax.slice_in_dim(block, 0, width, axis=dim), axis, backward)  3.5 us
  transfers between devices with their start and end apart: 6, of which 3 were waited for; matrix products, arithmetic and copies ran while one was open for 2% of the time, Pallas kernels for 0%

profile of v1, /device:TPU:21, one launch (start us, length us, event | category | flops | bytes accessed | tf_op | source)
XLA Modules:
  0.0 120.5 jit_solution(4268884716858692132)
XLA Ops:
  0.7 1.1 fusion.93
  1.8 3.3 %collective-permute-start = (bf16[1,1,16,16,256]{4,3,2,1,0:T(8,128)(2,1)S(1)}, bf16[1,1,16,16,256]{4,3,2,1,0:T(8,128)(2,1)S(1)}, u32[]{:S(2)}, u32[]{:S(2)}) collective-permute-start(bf16[1,1,16,16,256]{4,3,2,1,0:T(8,128)(2,1)S(1)} %get-tuple-element.42), channel_id=1, source_target_pairs={{0,1},{1,2},{2,3},{4,5},{5,6},{6,7},{8,9},{9,10},{10,11},{12,13},{... | collective-permute-start | bytes 393224 | tf_op jit(solution)/shard_map/ppermute | solution.py:23
  5.1 2.1 %collective-permute-start.1 = (bf16[1,1,16,16,256]{4,3,2,1,0:T(8,128)(2,1)S(1)}, bf16[1,1,16,16,256]{4,3,2,1,0:T(8,128)(2,1)S(1)}, u32[]{:S(2)}, u32[]{:S(2)}) collective-permute-start(bf16[1,1,16,16,256]{4,3,2,1,0:T(8,128)(2,1)S(1)} %get-tuple-element.43), channel_id=1, source_target_pairs={{1,0},{2,1},{3,2},{5,4},{6,5},{7,6},{9,8},{10,9},{11,10},{13,12},{... | collective-permute-start | bytes 393224 | tf_op jit(solution)/shard_map/ppermute | solution.py:26
  7.2 0.8 slice_bitcast_fusion.2
  8.0 0.8 slice_bitcast_fusion
  8.7 0.8 select_reduce_fusion.1
  9.6 1.3 %collective-permute-done.1 = bf16[1,1,16,16,256]{4,3,2,1,0:T(8,128)(2,1)S(1)} collective-permute-done((bf16[1,1,16,16,256]{4,3,2,1,0:T(8,128)(2,1)S(1)}, bf16[1,1,16,16,256]{4,3,2,1,0:T(8,128)(2,1)S(1)}, u32[]{:S(2)}, u32[]{:S(2)}) %collective-permute-start.1) | collective-permute-done | bytes 131104 | tf_op jit(solution)/shard_map/ppermute | solution.py:26
  10.9 1.0 maximum_bitcast_fusion
  11.9 0.3 pad_slice_fusion.1
  12.2 0.6 pad_slice_fusion
  19.5 0.8 copy-done.32
  20.5 0.7 slice.332
  21.2 0.7 slice.329
  21.9 2.1 %collective-permute-start.2 = (f32[1,16,16,2]{2,1,0,3:T(8,128)}, f32[1,16,16,2]{2,1,0,3:T(8,128)S(1)}, u32[]{:S(2)}, u32[]{:S(2)}) collective-permute-start(f32[1,16,16,2]{2,1,0,3:T(8,128)} %bitcast.55), channel_id=1, source_target_pairs={{1,0},{2,1},{3,2},{5,4},{6,5},{7,6},{9,8},{10,9},{11,10},{13,12},{... | collective-permute-start | bytes 6152 | tf_op jit(solution)/shard_map/ppermute | solution.py:26
  24.0 3.2 %collective-permute-start.3 = (f32[1,16,16,2]{2,1,0,3:T(8,128)}, f32[1,16,16,2]{2,1,0,3:T(8,128)S(1)}, u32[]{:S(2)}, u32[]{:S(2)}) collective-permute-start(f32[1,16,16,2]{2,1,0,3:T(8,128)} %bitcast.56), channel_id=1, source_target_pairs={{0,1},{1,2},{2,3},{4,5},{5,6},{6,7},{8,9},{9,10},{10,11},{12,13},{... | collective-permute-start | bytes 6152 | tf_op jit(solution)/shard_map/ppermute | solution.py:23
  27.3 1.3 %collective-permute-done.3 = f32[1,16,16,2]{2,1,0,3:T(8,128)S(1)} collective-permute-done((f32[1,16,16,2]{2,1,0,3:T(8,128)}, f32[1,16,16,2]{2,1,0,3:T(8,128)S(1)}, u32[]{:S(2)}, u32[]{:S(2)}) %collective-permute-start.3) | collective-permute-done | bytes 2080 | tf_op jit(solution)/shard_map/ppermute | solution.py:23
  28.9 3.2 %collective-permute-start.5 = (f32[1,16,16,2]{2,1,0,3:T(8,128)S(1)}, f32[1,16,16,2]{2,1,0,3:T(8,128)S(1)}, u32[]{:S(2)}, u32[]{:S(2)}) collective-permute-start(f32[1,16,16,2]{2,1,0,3:T(8,128)S(1)} %get-tuple-element.48), channel_id=1, source_target_pairs={{0,1},{1,2},{2,3},{4,5},{5,6},{6,7},{8,9},{9,10},{10,11},{12,13},{... | collective-permute-start | bytes 6152 | tf_op jit(solution)/shard_map/ppermute | solution.py:23
  32.1 2.3 %collective-permute-start.4 = (f32[1,16,16,2]{2,1,0,3:T(8,128)S(1)}, f32[1,16,16,2]{2,1,0,3:T(8,128)S(1)}, u32[]{:S(2)}, u32[]{:S(2)}) collective-permute-start(f32[1,16,16,2]{2,1,0,3:T(8,128)S(1)} %get-tuple-element.49), channel_id=1, source_target_pairs={{1,0},{2,1},{3,2},{5,4},{6,5},{7,6},{9,8},{10,9},{11,10},{13,12},{... | collective-permute-start | bytes 6152 | tf_op jit(solution)/shard_map/ppermute | solution.py:26
  34.4 2.2 %collective-permute-done.4 = f32[1,16,16,2]{2,1,0,3:T(8,128)S(1)} collective-permute-done((f32[1,16,16,2]{2,1,0,3:T(8,128)S(1)}, f32[1,16,16,2]{2,1,0,3:T(8,128)S(1)}, u32[]{:S(2)}, u32[]{:S(2)}) %collective-permute-start.4) | collective-permute-done | bytes 2080 | tf_op jit(solution)/shard_map/ppermute | solution.py:26
  37.1 1.7 %fusion.4 = bf16[512,256]{1,0:T(8,128)(2,1)S(1)} fusion(bf16[256,2]{0,1:T(2,128)(2,1)S(1)} %copy-done, f32[512,256]{1,0:T(8,128)} %copy-done.32, f32[512,1]{0,1:T(1,128)S(1)} %stack.16, f32[512,1]{0,1:T(1,128)S(1)} %stack.15), kind=kOutput, calls=%fused_computation.53 | convolution fusion | flops 4326400 | bytes 791552 | tf_op jit(solution)/shard_map/dot_general | solution.py:331
  39.0 1.2 %convolution_dynamic-update-slice_fusion.24 = f32[6912,256]{1,0:T(8,128)S(1)} fusion(f32[6912,256]{1,0:T(8,128)S(1)} %convolution_dynamic-update-slice_fusion.25, bf16[512,256]{1,0:T(8,128)(2,1)} %bitcast.338, bf16[512,256]{1,0:T(8,128)(2,1)S(1)} %fusion.4), kind=kOutput, calls=%fused_computation.78 | convolution fusion | flops 67108864 | bytes 786432 | tf_op jit(solution)/shard_map/dot_general | solution.py:337
  40.3 1.2 %convolution_dynamic-update-slice_fusion.23 = f32[6912,256]{1,0:T(8,128)S(1)} fusion(f32[6912,256]{1,0:T(8,128)S(1)} %convolution_dynamic-update-slice_fusion.24, bf16[512,256]{1,0:T(8,128)(2,1)} %bitcast.336, bf16[512,256]{1,0:T(8,128)(2,1)S(1)} %fusion.4), kind=kOutput, calls=%fused_computation.77 | convolution fusion | flops 67108864 | bytes 786432 | tf_op jit(solution)/shard_map/dot_general | solution.py:337
  41.5 1.2 %convolution_dynamic-update-slice_fusion.22 = f32[6912,256]{1,0:T(8,128)S(1)} fusion(f32[6912,256]{1,0:T(8,128)S(1)} %convolution_dynamic-update-slice_fusion.23, bf16[512,256]{1,0:T(8,128)(2,1)} %bitcast.334, bf16[512,256]{1,0:T(8,128)(2,1)S(1)} %fusion.4), kind=kOutput, calls=%fused_computation.76 | convolution fusion | flops 67108864 | bytes 786432 | tf_op jit(solution)/shard_map/dot_general | solution.py:337
  42.7 0.3 convolution_dynamic-update-slice_fusion.21
  43.0 0.3 convolution_dynamic-update-slice_fusion.20
  43.3 0.3 convolution_dynamic-update-slice_fusion.19
  43.6 0.3 convolution_dynamic-update-slice_fusion.18
  43.9 0.3 convolution_dynamic-update-slice_fusion.17
  44.2 0.3 convolution_dynamic-update-slice_fusion.16
  44.8 0.3 convolution_dynamic-update-slice_fusion.14
  45.1 0.3 convolution_dynamic-update-slice_fusion.13
  45.3 0.3 fusion.5
  45.6 0.3 convolution_dynamic-update-slice_fusion.12
  45.9 0.3 convolution_dynamic-update-slice_fusion.11
  46.2 0.3 convolution_dynamic-update-slice_fusion.10
  46.5 0.3 convolution_dynamic-update-slice_fusion.9
  46.8 0.3 convolution_dynamic-update-slice_fusion.8
  47.0 0.3 convolution_dynamic-update-slice_fusion.7
  47.3 0.3 convolution_dynamic-update-slice_fusion.6
  47.6 0.3 convolution_dynamic-update-slice_fusion.5
  47.9 0.3 convolution_dynamic-update-slice_fusion.4
  48.7 0.3 convolution_dynamic-update-slice_fusion.1
  49.3 2.8 %copy-done.4 = f32[6912,256]{1,0:T(8,128)} copy-done((f32[6912,256]{1,0:T(8,128)}, f32[6912,256]{1,0:T(8,128)S(1)}, u32[]{:S(2)}) %copy-start.4) | copy-done | bytes 7077912
  52.1 64.2 %shard_map.129 = (f32[432,128]{1,0:T(8,128)S(1)}, f32[432,128]{1,0:T(8,128)S(1)}, f32[432,128]{1,0:T(8,128)S(1)}, bf16[4,2,4,224,256]{4,3,2,1,0:T(8,128)(2,1)S(1)}) custom-call(f32[4,2,4,216,256]{4,3,2,1,0:T(8,128)} %bitcast.283, f32[432,128]{1,0:T(8,128)S(1)} %bitcast.280, f32[432,128]{1,0:T(8,128)S(1)} %bitcast.281, f32[432,128]{1,0:T(8,128)S(1)} %bitcast.282), custom_call_target="tpu_custom_call" | custom-call | tf_op jit(solution)/shard_map/pallas_call | solution.py:237
  116.3 2.1 %slice.356 = bf16[4,2,4,216,256]{4,3,2,1,0:T(8,128)(2,1)} slice(bf16[4,2,4,224,256]{4,3,2,1,0:T(8,128)(2,1)S(1)} %get-tuple-element.11), slice={[0:4], [0:2], [0:4], [0:216], [0:256]} | slice | bytes 7077888 | tf_op jit(solution)/shard_map/slice | solution.py:276
  118.4 0.7 copy.49
  119.1 0.7 copy.50
  119.8 0.7 copy.51
  (116 shorter events, 8.6 us)
Async XLA Ops:
  0.6 19.6 %copy-start = (bf16[256,2]{0,1:T(2,128)(2,1)S(1)}, bf16[256,2]{0,1:T(2,128)(2,1)}, u32[]{:S(2)}) copy-start(bf16[256,2]{0,1:T(2,128)(2,1)} %param.12) | copy-start | bytes 3076
  0.6 12.3 %copy-start.6 = (bf16[27,256,256]{2,1,0:T(8,128)(2,1)S(1)}, bf16[27,256,256]{2,1,0:T(8,128)(2,1)}, u32[]{:S(2)}) copy-start(bf16[27,256,256]{2,1,0:T(8,128)(2,1)} %param.11) | copy-start | bytes 10616836
  1.8 7.8 %collective-permute-start = (bf16[1,1,16,16,256]{4,3,2,1,0:T(8,128)(2,1)S(1)}, bf16[1,1,16,16,256]{4,3,2,1,0:T(8,128)(2,1)S(1)}, u32[]{:S(2)}, u32[]{:S(2)}) collective-permute-start(bf16[1,1,16,16,256]{4,3,2,1,0:T(8,128)(2,1)S(1)} %get-tuple-element.42), channel_id=1, source_target_pairs={{0,1},{1,2},{2,3},{4,5},{5,6},{6,7},{8,9},{9,10},{10,11},{12,13},{... | collective-permute-start | bytes 393224 | tf_op jit(solution)/shard_map/ppermute | solution.py:23
  5.1 5.7 %collective-permute-start.1 = (bf16[1,1,16,16,256]{4,3,2,1,0:T(8,128)(2,1)S(1)}, bf16[1,1,16,16,256]{4,3,2,1,0:T(8,128)(2,1)S(1)}, u32[]{:S(2)}, u32[]{:S(2)}) collective-permute-start(bf16[1,1,16,16,256]{4,3,2,1,0:T(8,128)(2,1)S(1)} %get-tuple-element.43), channel_id=1, source_target_pairs={{1,0},{2,1},{3,2},{5,4},{6,5},{7,6},{9,8},{10,9},{11,10},{13,12},{... | collective-permute-start | bytes 393224 | tf_op jit(solution)/shard_map/ppermute | solution.py:26
  11.9 2.5 %copy-start.5 = (bf16[1,2,16,16,256]{4,3,2,1,0:T(8,128)(2,1)S(1)}, bf16[1,2,16,16,256]{4,3,2,1,0:T(8,128)(2,1)}, u32[]{:S(2)}) copy-start(bf16[1,2,16,16,256]{4,3,2,1,0:T(8,128)(2,1)} %param.10) | copy-start | bytes 786436
  12.8 1.3 %copy-start.29 = (bf16[2,16,16,256]{3,2,1,0:T(8,128)(2,1)}, bf16[2,16,16,256]{3,2,1,0:T(8,128)(2,1)S(1)}, u32[]{:S(2)}) copy-start(bf16[2,16,16,256]{3,2,1,0:T(8,128)(2,1)S(1)} %get-tuple-element.19) | copy-start | bytes 786436
  12.8 2.5 %copy-start.23 = (bf16[2,16,16,256]{3,2,1,0:T(8,128)(2,1)}, bf16[2,16,16,256]{3,2,1,0:T(8,128)(2,1)S(1)}, u32[]{:S(2)}) copy-start(bf16[2,16,16,256]{3,2,1,0:T(8,128)(2,1)S(1)} %get-tuple-element.23) | copy-start | bytes 786436
  12.8 2.5 %copy-start.25 = (bf16[2,16,16,256]{3,2,1,0:T(8,128)(2,1)}, bf16[2,16,16,256]{3,2,1,0:T(8,128)(2,1)S(1)}, u32[]{:S(2)}) copy-start(bf16[2,16,16,256]{3,2,1,0:T(8,128)(2,1)S(1)} %get-tuple-element.22) | copy-start | bytes 786436
  12.9 2.5 %copy-start.27 = (bf16[2,16,16,256]{3,2,1,0:T(8,128)(2,1)}, bf16[2,16,16,256]{3,2,1,0:T(8,128)(2,1)S(1)}, u32[]{:S(2)}) copy-start(bf16[2,16,16,256]{3,2,1,0:T(8,128)(2,1)S(1)} %get-tuple-element.21) | copy-start | bytes 786436
  12.9 2.5 %copy-start.30 = (bf16[2,16,16,256]{3,2,1,0:T(8,128)(2,1)}, bf16[2,16,16,256]{3,2,1,0:T(8,128)(2,1)S(1)}, u32[]{:S(2)}) copy-start(bf16[2,16,16,256]{3,2,1,0:T(8,128)(2,1)S(1)} %get-tuple-element.18) | copy-start | bytes 786436
  12.9 2.5 %copy-start.31 = (bf16[2,16,16,256]{3,2,1,0:T(8,128)(2,1)}, bf16[2,16,16,256]{3,2,1,0:T(8,128)(2,1)S(1)}, u32[]{:S(2)}) copy-start(bf16[2,16,16,256]{3,2,1,0:T(8,128)(2,1)S(1)} %get-tuple-element.17) | copy-start | bytes 786436
  12.9 2.5 %copy-start.21 = (bf16[2,16,16,256]{3,2,1,0:T(8,128)(2,1)}, bf16[2,16,16,256]{3,2,1,0:T(8,128)(2,1)S(1)}, u32[]{:S(2)}) copy-start(bf16[2,16,16,256]{3,2,1,0:T(8,128)(2,1)S(1)} %get-tuple-element.24) | copy-start | bytes 786436
  12.9 2.8 %copy-start.19 = (bf16[2,16,16,256]{3,2,1,0:T(8,128)(2,1)}, bf16[2,16,16,256]{3,2,1,0:T(8,128)(2,1)S(1)}, u32[]{:S(2)}) copy-start(bf16[2,16,16,256]{3,2,1,0:T(8,128)(2,1)S(1)} %get-tuple-element.25) | copy-start | bytes 786436
  12.9 3.0 %copy-start.17 = (bf16[2,16,16,256]{3,2,1,0:T(8,128)(2,1)}, bf16[2,16,16,256]{3,2,1,0:T(8,128)(2,1)S(1)}, u32[]{:S(2)}) copy-start(bf16[2,16,16,256]{3,2,1,0:T(8,128)(2,1)S(1)} %get-tuple-element.26) | copy-start | bytes 786436
  12.9 3.2 %copy-start.15 = (bf16[2,16,16,256]{3,2,1,0:T(8,128)(2,1)}, bf16[2,16,16,256]{3,2,1,0:T(8,128)(2,1)S(1)}, u32[]{:S(2)}) copy-start(bf16[2,16,16,256]{3,2,1,0:T(8,128)(2,1)S(1)} %get-tuple-element.27) | copy-start | bytes 786436
  12.9 3.7 %copy-start.13 = (bf16[2,16,16,256]{3,2,1,0:T(8,128)(2,1)}, bf16[2,16,16,256]{3,2,1,0:T(8,128)(2,1)S(1)}, u32[]{:S(2)}) copy-start(bf16[2,16,16,256]{3,2,1,0:T(8,128)(2,1)S(1)} %get-tuple-element.28) | copy-start | bytes 786436
  12.9 3.9 %copy-start.11 = (bf16[2,16,16,256]{3,2,1,0:T(8,128)(2,1)}, bf16[2,16,16,256]{3,2,1,0:T(8,128)(2,1)S(1)}, u32[]{:S(2)}) copy-start(bf16[2,16,16,256]{3,2,1,0:T(8,128)(2,1)S(1)} %get-tuple-element.29) | copy-start | bytes 786436
  12.9 4.1 %copy-start.9 = (bf16[2,16,16,256]{3,2,1,0:T(8,128)(2,1)}, bf16[2,16,16,256]{3,2,1,0:T(8,128)(2,1)S(1)}, u32[]{:S(2)}) copy-start(bf16[2,16,16,256]{3,2,1,0:T(8,128)(2,1)S(1)} %get-tuple-element.30) | copy-start | bytes 786436
  13.0 4.4 %copy-start.7 = (bf16[2,16,16,256]{3,2,1,0:T(8,128)(2,1)}, bf16[2,16,16,256]{3,2,1,0:T(8,128)(2,1)S(1)}, u32[]{:S(2)}) copy-start(bf16[2,16,16,256]{3,2,1,0:T(8,128)(2,1)S(1)} %get-tuple-element.31) | copy-start | bytes 786436
  17.6 9.6 %copy-start.33 = (s32[1,2,16,16]{3,2,1,0:T(8,128)S(1)}, s32[1,2,16,16]{3,2,1,0:T(8,128)}, u32[]{:S(2)}) copy-start(s32[1,2,16,16]{3,2,1,0:T(8,128)} %param.14) | copy-start | bytes 6148
  19.5 0.8 copy-start.32
  21.9 5.5 %collective-permute-start.2 = (f32[1,16,16,2]{2,1,0,3:T(8,128)}, f32[1,16,16,2]{2,1,0,3:T(8,128)S(1)}, u32[]{:S(2)}, u32[]{:S(2)}) collective-permute-start(f32[1,16,16,2]{2,1,0,3:T(8,128)} %bitcast.55), channel_id=1, source_target_pairs={{1,0},{2,1},{3,2},{5,4},{6,5},{7,6},{9,8},{10,9},{11,10},{13,12},{... | collective-permute-start | bytes 6152 | tf_op jit(solution)/shard_map/ppermute | solution.py:26
  24.0 4.7 %collective-permute-start.3 = (f32[1,16,16,2]{2,1,0,3:T(8,128)}, f32[1,16,16,2]{2,1,0,3:T(8,128)S(1)}, u32[]{:S(2)}, u32[]{:S(2)}) collective-permute-start(f32[1,16,16,2]{2,1,0,3:T(8,128)} %bitcast.56), channel_id=1, source_target_pairs={{0,1},{1,2},{2,3},{4,5},{5,6},{6,7},{8,9},{9,10},{10,11},{12,13},{... | collective-permute-start | bytes 6152 | tf_op jit(solution)/shard_map/ppermute | solution.py:23
  28.9 5.5 %collective-permute-start.5 = (f32[1,16,16,2]{2,1,0,3:T(8,128)S(1)}, f32[1,16,16,2]{2,1,0,3:T(8,128)S(1)}, u32[]{:S(2)}, u32[]{:S(2)}) collective-permute-start(f32[1,16,16,2]{2,1,0,3:T(8,128)S(1)} %get-tuple-element.48), channel_id=1, source_target_pairs={{0,1},{1,2},{2,3},{4,5},{5,6},{6,7},{8,9},{9,10},{10,11},{12,13},{... | collective-permute-start | bytes 6152 | tf_op jit(solution)/shard_map/ppermute | solution.py:23
  32.1 4.5 %collective-permute-start.4 = (f32[1,16,16,2]{2,1,0,3:T(8,128)S(1)}, f32[1,16,16,2]{2,1,0,3:T(8,128)S(1)}, u32[]{:S(2)}, u32[]{:S(2)}) collective-permute-start(f32[1,16,16,2]{2,1,0,3:T(8,128)S(1)} %get-tuple-element.49), channel_id=1, source_target_pairs={{1,0},{2,1},{3,2},{5,4},{6,5},{7,6},{9,8},{10,9},{11,10},{13,12},{... | collective-permute-start | bytes 6152 | tf_op jit(solution)/shard_map/ppermute | solution.py:26
  37.0 6.3 %copy-start.28 = (bf16[2,16,16,256]{3,2,1,0:T(8,128)(2,1)S(1)}, bf16[2,16,16,256]{3,2,1,0:T(8,128)(2,1)}, u32[]{:S(2)}) copy-start(bf16[2,16,16,256]{3,2,1,0:T(8,128)(2,1)} %copy-done.27) | copy-start | bytes 786436
  37.0 6.6 %copy-start.26 = (bf16[2,16,16,256]{3,2,1,0:T(8,128)(2,1)S(1)}, bf16[2,16,16,256]{3,2,1,0:T(8,128)(2,1)}, u32[]{:S(2)}) copy-start(bf16[2,16,16,256]{3,2,1,0:T(8,128)(2,1)} %copy-done.25) | copy-start | bytes 786436
  37.0 6.9 %copy-start.24 = (bf16[2,16,16,256]{3,2,1,0:T(8,128)(2,1)S(1)}, bf16[2,16,16,256]{3,2,1,0:T(8,128)(2,1)}, u32[]{:S(2)}) copy-start(bf16[2,16,16,256]{3,2,1,0:T(8,128)(2,1)} %copy-done.23) | copy-start | bytes 786436
  37.0 7.1 %copy-start.22 = (bf16[2,16,16,256]{3,2,1,0:T(8,128)(2,1)S(1)}, bf16[2,16,16,256]{3,2,1,0:T(8,128)(2,1)}, u32[]{:S(2)}) copy-start(bf16[2,16,16,256]{3,2,1,0:T(8,128)(2,1)} %copy-done.21) | copy-start | bytes 786436
  37.0 7.5 %copy-start.20 = (bf16[2,16,16,256]{3,2,1,0:T(8,128)(2,1)S(1)}, bf16[2,16,16,256]{3,2,1,0:T(8,128)(2,1)}, u32[]{:S(2)}) copy-start(bf16[2,16,16,256]{3,2,1,0:T(8,128)(2,1)} %copy-done.19) | copy-start | bytes 786436
  37.0 7.7 %copy-start.18 = (bf16[2,16,16,256]{3,2,1,0:T(8,128)(2,1)S(1)}, bf16[2,16,16,256]{3,2,1,0:T(8,128)(2,1)}, u32[]{:S(2)}) copy-start(bf16[2,16,16,256]{3,2,1,0:T(8,128)(2,1)} %copy-done.17) | copy-start | bytes 786436
  37.0 8.0 %copy-start.16 = (bf16[2,16,16,256]{3,2,1,0:T(8,128)(2,1)S(1)}, bf16[2,16,16,256]{3,2,1,0:T(8,128)(2,1)}, u32[]{:S(2)}) copy-start(bf16[2,16,16,256]{3,2,1,0:T(8,128)(2,1)} %copy-done.15) | copy-start | bytes 786436
  37.0 8.6 %copy-start.14 = (bf16[2,16,16,256]{3,2,1,0:T(8,128)(2,1)S(1)}, bf16[2,16,16,256]{3,2,1,0:T(8,128)(2,1)}, u32[]{:S(2)}) copy-start(bf16[2,16,16,256]{3,2,1,0:T(8,128)(2,1)} %copy-done.13) | copy-start | bytes 786436
  37.1 8.9 %copy-start.12 = (bf16[2,16,16,256]{3,2,1,0:T(8,128)(2,1)S(1)}, bf16[2,16,16,256]{3,2,1,0:T(8,128)(2,1)}, u32[]{:S(2)}) copy-start(bf16[2,16,16,256]{3,2,1,0:T(8,128)(2,1)} %copy-done.11) | copy-start | bytes 786436
  37.1 9.1 %copy-start.10 = (bf16[2,16,16,256]{3,2,1,0:T(8,128)(2,1)S(1)}, bf16[2,16,16,256]{3,2,1,0:T(8,128)(2,1)}, u32[]{:S(2)}) copy-start(bf16[2,16,16,256]{3,2,1,0:T(8,128)(2,1)} %copy-done.9) | copy-start | bytes 786436
  38.8 7.7 %copy-start.8 = (bf16[2,16,16,256]{3,2,1,0:T(8,128)(2,1)S(1)}, bf16[2,16,16,256]{3,2,1,0:T(8,128)(2,1)}, u32[]{:S(2)}) copy-start(bf16[2,16,16,256]{3,2,1,0:T(8,128)(2,1)} %copy-done.7) | copy-start | bytes 786436
  44.2 8.0 %copy-start.1 = (f32[55296]{0:T(1024)S(1)}, f32[55296]{0:T(1024)}, u32[]{:S(2)}) copy-start(f32[55296]{0:T(1024)} %param.17) | copy-start | bytes 663556
  44.2 8.0 %copy-start.2 = (f32[55296]{0:T(1024)S(1)}, f32[55296]{0:T(1024)}, u32[]{:S(2)}) copy-start(f32[55296]{0:T(1024)} %param.18) | copy-start | bytes 663556
  44.2 8.0 %copy-start.3 = (f32[55296]{0:T(1024)S(1)}, f32[55296]{0:T(1024)}, u32[]{:S(2)}) copy-start(f32[55296]{0:T(1024)} %param.19) | copy-start | bytes 663556
  49.3 2.9 %copy-start.4 = (f32[6912,256]{1,0:T(8,128)}, f32[6912,256]{1,0:T(8,128)S(1)}, u32[]{:S(2)}) copy-start(f32[6912,256]{1,0:T(8,128)S(1)} %convolution_dynamic-update-slice_fusion) | copy-start | bytes 21233668

commit v2 on v1

--- a/solution.py
+++ b/solution.py
@@ -15,35 +15,262 @@
 adam_eps = 1e-08
 
 
-def padded_2(block, sides, width):
-    for axis, dim in sides:
-        count = lax.axis_size(axis)
-        forward = [(i, i + 1) for i in range(count - 1)]
-        backward = [(target, source) for source, target in forward]
-        low = lax.ppermute(
-            lax.slice_in_dim(block, block.shape[dim] - width, None, axis=dim), axis, forward
-        )
-        high = lax.ppermute(lax.slice_in_dim(block, 0, width, axis=dim), axis, backward)
-        block = jnp.concatenate([low, block, high], axis=dim)
-    return block
-
-
-def laplace(extended):
-    padded = jnp.pad(extended, ((0, 0), (1, 1), (1, 1), (0, 0)))
-    centre = padded[1:-1, 1:-1, 1:-1]
-    near = padded[2:, 1:-1, 1:-1] + padded[:-2, 1:-1, 1:-1]
-    near = near + padded[1:-1, 2:, 1:-1] + padded[1:-1, :-2, 1:-1]
-    near = near + padded[1:-1, 1:-1, 2:] + padded[1:-1, 1:-1, :-2]
-    return near - 6.0 * centre
-
-
-def lookup(codes, table, offset):
-    count = table.shape[1]
-    values = jnp.arange(count, dtype=jnp.int32) + offset
-    hits = codes[..., None] == values
-    real_part = jnp.sum(jnp.where(hits, table[0], 0.0), axis=-1)
-    imag_part = jnp.sum(jnp.where(hits, table[1], 0.0), axis=-1)
-    return (real_part, imag_part)
+def spread(values, table, first):
+    real = jnp.zeros(values.shape, jnp.float32)
+    imag = jnp.zeros(values.shape, jnp.float32)
+    for entry in range(table.shape[1]):
+        hit = values == entry + first
+        real = jnp.where(hit, table[0, entry], real)
+        imag = jnp.where(hit, table[1, entry], imag)
+    return real, imag
+
+
+def grad_kernel(
+    sizes,
+    scale,
+    norm_scale,
+    features,
+    weights,
+    head,
+    materials,
+    ports,
+    permittivity,
+    port_source,
+    grad,
+    halo,
+    near_taps,
+    turned,
+    factor,
+    d_pad,
+    edge_out,
+    edge_in,
+    send,
+    recv,
+):
+    line, grid_w = sizes
+    depth, cells, channels = features.shape
+    wide = 3 * channels
+    dp = lax.axis_index("dp")
+    here = lax.axis_index("slab")
+    has_low = here > 0
+    has_high = here < line - 1
+    low = (dp, here - 1)
+    high = (dp, here + 1)
+
+    def remote(source, target, stage, way, device):
+        return pltpu.make_async_remote_copy(
+            src_ref=source,
+            dst_ref=target,
+            send_sem=send.at[stage, way],
+            recv_sem=recv.at[stage, way],
+            device_id=device,
+            device_id_type=pl.DeviceIdType.MESH,
+        )
+
+    def sends(stage):
+        if stage == 0:
+            return (
+                remote(features.at[0], halo.at[1], 0, 1, low),
+                remote(features.at[depth - 1], halo.at[0], 0, 0, high),
+            )
+        return (
+            remote(edge_out.at[stage - 1, 0], edge_in.at[stage - 1, 1], stage, 1, low),
+            remote(edge_out.at[stage - 1, 1], edge_in.at[stage - 1, 0], stage, 0, high),
+        )
+
+    def start(stage):
+        to_low, to_high = sends(stage)
+        pl.when(has_low)(to_low.start)
+        pl.when(has_high)(to_high.start)
+
+    def finish(stage):
+        to_low, to_high = sends(stage)
+        pl.when(has_low)(to_high.wait_recv)
+        pl.when(has_high)(to_low.wait_recv)
+        pl.when(has_low)(to_low.wait_send)
+        pl.when(has_high)(to_high.wait_send)
+
+    barrier = pltpu.get_barrier_semaphore()
+    for there, device in ((has_low, low), (has_high, high)):
+
+        @pl.when(there)
+        def _(device=device):
+            pl.semaphore_signal(
+                barrier, inc=1, device_id=device, device_id_type=pl.DeviceIdType.MESH
+            )
+
+    pl.semaphore_wait(barrier, jnp.where(has_low, 1, 0) + jnp.where(has_high, 1, 0))
+
+    start(0)
+    for side, there in ((0, has_low), (1, has_high)):
+
+        @pl.when(jnp.logical_not(there))
+        def _(side=side):
+            halo[side] = jnp.zeros((cells, channels), jnp.bfloat16)
+            for stage in range(2):
+                edge_in[stage, side] = jnp.zeros((8, cells), jnp.float32)
+
+    empty = jnp.zeros((grid_w, wide), jnp.bfloat16)
+    for plane in range(depth + 2):
+        near_taps[plane, :grid_w] = empty
+        near_taps[plane, grid_w + cells :] = empty
+    for plane in range(depth):
+        d_pad[plane, :grid_w] = empty[:, :channels]
+        d_pad[plane, grid_w + cells :] = empty[:, :channels]
+
+    column = lax.broadcasted_iota(jnp.int32, (cells, channels), 0) % grid_w
+
+    def lay(plane, block):
+        body_rows = pl.ds(grid_w, cells)
+        values = block.astype(jnp.float32)
+        before = jnp.where(column == 0, 0.0, pltpu.roll(values, 1, 0))
+        after = jnp.where(column == grid_w - 1, 0.0, pltpu.roll(values, cells - 1, 0))
+        near_taps[plane, body_rows, :channels] = before.astype(jnp.bfloat16)
+        near_taps[plane, body_rows, channels : 2 * channels] = block
+        near_taps[plane, body_rows, 2 * channels :] = after.astype(jnp.bfloat16)
+
+    def taps(shift_z):
+        total = None
+        for shift_y in range(3):
+            rows = near_taps[shift_z : shift_z + depth, shift_y * grid_w : shift_y * grid_w + cells]
+            first = 9 * shift_z + 3 * shift_y
+            part = jnp.dot(
+                rows.reshape(depth * cells, wide),
+                weights[first : first + 3].reshape(wide, channels),
+                preferred_element_type=jnp.float32,
+            )
+            total = part if total is None else total + part
+        return total
+
+    def turn(plane):
+        turned[:, plane * cells : (plane + 1) * cells] = near_taps[plane, grid_w : grid_w + cells].T
+
+    for plane in range(depth):
+        lay(plane + 1, features[plane])
+    factor[...] = taps(1)
+    finish(0)
+    lay(0, halo[0])
+    lay(depth + 1, halo[1])
+    factor[...] += taps(0)
+    preact = (factor[...] + taps(2)) * scale
+    sigma = 1.0 / (1.0 + jnp.exp(-preact))
+    hidden = (preact * sigma).astype(jnp.bfloat16)
+    factor[...] = sigma * (1.0 + preact * (1.0 - sigma))
+    field_rows = lax.dot_general(
+        head[...], hidden, (((1,), (1,)), ((), ())), preferred_element_type=jnp.float32
+    )[:8]
+    field = [field_rows[:, plane * cells : (plane + 1) * cells] for plane in range(depth)]
+
+    lane = lax.broadcasted_iota(jnp.int32, (8, cells), 1)
+    row = lax.broadcasted_iota(jnp.int32, (8, cells), 0)
+    lane_x = lane % grid_w
+
+    def exchange(stage, planes):
+        edge_out[stage - 1, 0] = planes[0]
+        edge_out[stage - 1, 1] = planes[depth - 1]
+        start(stage)
+
+    def laplace(stage, planes):
+        around = [edge_in[stage - 1, 0]] + planes + [edge_in[stage - 1, 1]]
+        out = []
+        for plane in range(depth):
+            centre = planes[plane]
+            near = around[plane] + around[plane + 2]
+            near = near + jnp.where(lane < grid_w, 0.0, pltpu.roll(centre, grid_w, 1))
+            near = near + jnp.where(
+                lane >= cells - grid_w, 0.0, pltpu.roll(centre, cells - grid_w, 1)
+            )
+            near = near + jnp.where(lane_x == 0, 0.0, pltpu.roll(centre, 1, 1))
+            near = near + jnp.where(lane_x == grid_w - 1, 0.0, pltpu.roll(centre, cells - 1, 1))
+            out.append(near - 6.0 * centre)
+        return out
+
+    def both(real, imag):
+        shape = (8, cells)
+        imag = jnp.where(row == 1, jnp.broadcast_to(imag, shape), 0.0)
+        return jnp.where(row == 0, jnp.broadcast_to(real, shape), imag)
+
+    exchange(1, field)
+    for plane in range(1, depth + 1):
+        turn(plane)
+    eps = [spread(materials[plane : plane + 1], permittivity, 0) for plane in range(depth)]
+    src = [spread(ports[plane : plane + 1], port_source, 1) for plane in range(depth)]
+    finish(1)
+    adjoint = []
+    for plane, lap in enumerate(laplace(1, field)):
+        real, imag = field[plane][0:1], field[plane][1:2]
+        eps_re, eps_im = eps[plane]
+        src_re, src_im = src[plane]
+        local = both(
+            wave_sq * (eps_re * real - eps_im * imag) - src_re,
+            wave_sq * (eps_re * imag + eps_im * real) - src_im,
+        )
+        adjoint.append((lap + local) * norm_scale)
+    exchange(2, adjoint)
+    turn(0)
+    turn(depth + 1)
+    finish(2)
+    for plane, lap in enumerate(laplace(2, adjoint)):
+        real, imag = adjoint[plane][0:1], adjoint[plane][1:2]
+        eps_re, eps_im = eps[plane]
+        back = lap + both(
+            wave_sq * (eps_re * real + eps_im * imag), wave_sq * (eps_re * imag - eps_im * real)
+        )
+        columns = back.T
+        projection = head[...].astype(jnp.float32)
+        d_hidden = columns[:, 0:1] * projection[0:1] + columns[:, 1:2] * projection[1:2]
+        d_pre = d_hidden * factor[plane * cells : (plane + 1) * cells]
+        d_pad[plane, grid_w : grid_w + cells] = d_pre.astype(jnp.bfloat16)
+
+    for shift_z in range(3):
+        left = turned[:, shift_z * cells : (shift_z + depth) * cells]
+        for shift_y in range(3):
+            top = (2 - shift_y) * grid_w
+            first = 9 * shift_z + 3 * shift_y
+            grad[first : first + 3] = jnp.dot(
+                left,
+                d_pad[:, top : top + cells].reshape(depth * cells, channels),
+                preferred_element_type=jnp.float32,
+            ).reshape(3, channels, channels)
+
+
+def local_grad(features, weights, head_proj, materials, ports, permittivity, port_source, scale):
+    depth, grid_h, grid_w, channels = features.shape
+    cells = grid_h * grid_w
+    line = lax.axis_size("slab")
+    all_cells = depth * cells * lax.axis_size("dp") * line
+    norm_scale = float(np.float32(2.0) / np.sqrt(np.float32(all_cells)))
+    vmem = pl.BlockSpec(memory_space=pltpu.VMEM)
+    smem = pl.BlockSpec(memory_space=pltpu.SMEM)
+    tall = cells + 2 * grid_w
+    return pl.pallas_call(
+        functools.partial(grad_kernel, (line, grid_w), scale, norm_scale),
+        out_shape=jax.ShapeDtypeStruct((27, channels, channels), jnp.float32),
+        in_specs=[vmem] * 5 + [smem] * 2,
+        out_specs=vmem,
+        scratch_shapes=[
+            pltpu.VMEM((2, cells, channels), jnp.bfloat16),
+            pltpu.VMEM((depth + 2, tall, 3 * channels), jnp.bfloat16),
+            pltpu.VMEM((3 * channels, (depth + 2) * cells), jnp.bfloat16),
+            pltpu.VMEM((depth * cells, channels), jnp.float32),
+            pltpu.VMEM((depth, tall, channels), jnp.bfloat16),
+            pltpu.VMEM((2, 2, 8, cells), jnp.float32),
+            pltpu.VMEM((2, 2, 8, cells), jnp.float32),
+            pltpu.SemaphoreType.DMA((3, 2)),
+            pltpu.SemaphoreType.DMA((3, 2)),
+        ],
+        compiler_params=pltpu.CompilerParams(
+            collective_id=1, has_side_effects=True, vmem_limit_bytes=48 * 1024 * 1024
+        ),
+    )(
+        features.reshape(depth, cells, channels),
+        weights,
+        jnp.pad(head_proj.T, ((0, 14), (0, 0))),
+        materials.reshape(depth, cells),
+        ports.reshape(depth, cells),
+        permittivity,
+        port_source,
+    )
 
 
 def widen(block, rows):
@@ -289,60 +516,18 @@
     moment,
     second,
 ):
-    feats = features[0]
-    slab_depth, grid_rows, grid_cols, channels = feats.shape
-    cell_count = slab_depth * grid_rows * grid_cols
-    all_cells = cell_count * lax.axis_size("dp") * lax.axis_size("slab")
-    weight_scale = 1.0 / jnp.sqrt(jnp.float32(27 * channels))
-    with_rim = padded_2(features, (("slab", 1),), 1)[0]
-    padded = jnp.pad(with_rim, ((0, 0), (1, 1), (1, 1), (0, 0)))
-    pieces = []
-    summed = jnp.zeros((cell_count, channels), jnp.float32)
-    for tap_index in range(27):
-        shift_z, shift_y, shift_x = (tap_index // 9, tap_index // 3 % 3, tap_index % 3)
-        partial_rows = padded[
-            shift_z : shift_z + slab_depth,
-            shift_y : shift_y + grid_rows,
-            shift_x : shift_x + grid_cols,
-        ].reshape(cell_count, channels)
-        pieces.append(partial_rows)
-        summed = summed + jnp.dot(
-            partial_rows, kernel[tap_index], preferred_element_type=jnp.float32
-        )
-    preact = summed * weight_scale
-    hidden = jax.nn.silu(preact).astype(jnp.bfloat16)
-    field_vals = jnp.dot(hidden, head_proj, preferred_element_type=jnp.float32).reshape(
-        slab_depth, grid_rows, grid_cols, 2
-    )
-    eps_re, eps_im = lookup(material_ids[0], permittivity, 0)
-    src_re, src_im = lookup(port_ids[0], port_source, 1)
-    field_ext = padded_2(field_vals, (("slab", 0),), 1)
-    lap_field = laplace(field_ext)
-    field_re, field_im = (field_vals[..., 0], field_vals[..., 1])
-    res_re = lap_field[..., 0] + wave_sq * (eps_re * field_re - eps_im * field_im) - src_re
-    res_im = lap_field[..., 1] + wave_sq * (eps_re * field_im + eps_im * field_re) - src_im
-    norm_scale = 2.0 / jnp.sqrt(jnp.float32(all_cells))
-    adjoint = jnp.stack([res_re * norm_scale, res_im * norm_scale], axis=-1)
-    adj_ext = padded_2(adjoint, (("slab", 0),), 1)
-    lap_adj = laplace(adj_ext)
-    grad_re = lap_adj[..., 0] + wave_sq * (eps_re * adjoint[..., 0] + eps_im * adjoint[..., 1])
-    grad_im = lap_adj[..., 1] + wave_sq * (eps_re * adjoint[..., 1] - eps_im * adjoint[..., 0])
-    grad_field = jnp.stack([grad_re, grad_im], axis=-1).reshape(cell_count, 2)
-    d_hidden = jnp.dot(grad_field, head_proj.astype(jnp.float32).T, precision=lax.Precision.HIGHEST)
-    sigma = jax.nn.sigmoid(preact)
-    d_pre = (d_hidden * sigma * (1.0 + preact * (1.0 - sigma))).astype(jnp.bfloat16)
-    grads = []
-    for tap_index in range(27):
-        grads.append(
-            lax.dot_general(
-                pieces[tap_index],
-                d_pre,
-                (((0,), (0,)), ((), ())),
-                preferred_element_type=jnp.float32,
-            )
-        )
-    grad = jnp.concatenate(grads, axis=0)
+    channels = features.shape[-1]
     scale = float(np.float32(1.0) / np.sqrt(np.float32(27 * channels)))
+    grad = local_grad(
+        features[0],
+        kernel,
+        head_proj,
+        material_ids[0],
+        port_ids[0],
+        permittivity,
+        port_source,
+        scale,
+    ).reshape(27 * channels, channels)
     new_master, new_moment, new_second, full = share_and_step(grad, master, moment, second, scale)
     new_kernel = full.reshape(kernel.shape)
     return (new_master, new_moment, new_second, new_kernel)

time: 121 us -> 93.6 us (0.77)
  matrix products: 18.2 us -> 0 us
  Pallas kernels: 64.2 us -> 81.2 us
  starting transfers between devices: 16.1 us -> 0 us
  waiting for transfers between devices: 4.81 us -> 0 us
  local copies, waits for them, and re-layouts: 13.2 us -> 10.8 us
  other arithmetic: 2.36 us -> 0 us
    pallas_call x0 -> x1, Pallas kernels: none -> 18.6 us  [local_grad(): pl.pallas_call(functools.partial(grad_kernel, (line, grid_w), scale, norm...]
    dot_general x56 -> x0, matrix products: 18.2 us -> none  [the longest x27 10.2 us: body(): lax.dot_general(pieces[tap_index], d_pre, (((0,), (0,)), ((), ())), prefe...]
    ppermute x6 -> x0, starting transfers between devices: 16.1 us -> none  [the longest x3 9.74 us: padded_2(): lax.ppermute(lax.slice_in_dim(block, block.shape[dim] - width, None, axis...]
    ppermute x6 -> x0, waiting for transfers between devices: 4.81 us -> none  [the longest x3 3.5 us: padded_2(): lax.ppermute(lax.slice_in_dim(block, 0, width, axis=dim), axis, backward)]
    slice x6 -> x0, local copies, waits for them, and re-layouts: 3.45 us -> none  [the longest x3 1.84 us: padded_2(): lax.slice_in_dim(block, block.shape[dim] - width, None, axis=dim)]
    pallas_call x1, Pallas kernels: 64.2 us -> 62.6 us  [share_and_step(): pl.pallas_call(functools.partial(share_kernel, scale), out_shape=[state,...]
    squeeze x2 -> x0, local copies, waits for them, and re-layouts: 1.52 us -> none  [lookup(): imag_part = jnp.sum(jnp.where(hits, table[1], 0.0), axis=-1)]
    another operation x2, local copies, waits for them, and re-layouts: 0.16 us -> 1.6 us  [the longest x1 0.8 us: local_grad(): ports.reshape(depth, cells)]
  transfers between devices with their start and end apart: 6 -> 0, of which waited for: 3 -> 0; matrix products, arithmetic and copies ran while one was open for 2% -> 0% of each run, Pallas kernels for 0% -> 0%
where the time goes in v2:
time: 93.6 us; the launch traced here: 92.7 us
  Pallas kernels  81.2 us (87%)
  local copies, waits for them, and re-layouts  10.8 us (12%)
    pallas_call x1, Pallas kernels, share_and_step(): pl.pallas_call(functools.partial(share_kernel, scale), out_shape=[state,...  62.6 us
    pallas_call x1, Pallas kernels, local_grad(): pl.pallas_call(functools.partial(grad_kernel, (line, grid_w), scale, norm...  18.6 us
    unnamed x17, local copies, waits for them, and re-layouts  6.42 us
    slice x1, local copies, waits for them, and re-layouts, share_and_step(): full = out[3][:, :, :, :rows].reshape(rows_all, width)  2.08 us

profile of v2, /device:TPU:21, one launch (start us, length us, event | category | flops | bytes accessed | tf_op | source)
XLA Modules:
  0.0 92.7 jit_solution(1067925828214050514)
XLA Ops:
  0.6 0.8 reshape_squeeze.10.materials
  1.4 0.8 reshape_squeeze.11.ports
  2.2 0.7 pad.4.head
  2.9 0.0 copy-start
  2.9 2.0 %copy-done = bf16[27,256,256]{2,1,0:T(8,128)(2,1)S(1)} copy-done((bf16[27,256,256]{2,1,0:T(8,128)(2,1)S(1)}, bf16[27,256,256]{2,1,0:T(8,128)(2,1)}, u32[]{:S(2)}) %copy-start) | copy-done | bytes 3538968
  4.9 0.0 copy-start.1
  4.9 0.9 %copy-done.1 = bf16[1,2,16,16,256]{4,3,2,1,0:T(8,128)(2,1)S(1)} copy-done((bf16[1,2,16,16,256]{4,3,2,1,0:T(8,128)(2,1)S(1)}, bf16[1,2,16,16,256]{4,3,2,1,0:T(8,128)(2,1)}, u32[]{:S(2)}) %copy-start.1) | copy-done | bytes 262168
  5.9 0.0 copy-start.5
  5.9 0.7 copy-done.5
  6.5 0.0 copy-start.6
  6.6 0.7 copy-done.6
  7.2 0.0 copy-start.2
  7.2 0.0 copy-start.3
  7.2 0.0 copy-start.4
  7.2 18.6 %shard_map.129 = f32[27,256,256]{2,1,0:T(8,128)} custom-call(bf16[2,256,256]{2,1,0:T(8,128)(2,1)S(1)} %bitcast.14, bf16[27,256,256]{2,1,0:T(8,128)(2,1)S(1)} %copy-done, bf16[16,256]{1,0:T(8,128)(2,1)S(1)} %pad.4.head, s32[2,256]{1,0:T(2,128)S(1)} %reshape_squeeze.10.materials, s32[2,256]{1,0:T(2,128)S(1)} %reshape_squeeze.11.ports, f32[2,4]{1,0:T(2,128)S(1)} %copy-done.5, ...), custom_call_target="tpu_custom_call" | custom-call | tf_op jit(solution)/shard_map/pallas_call | solution.py:246
  25.8 0.0 copy-done.2
  25.8 0.0 copy-done.3
  25.8 0.0 copy-done.4
  25.8 62.6 %shard_map.130 = (f32[432,128]{1,0:T(8,128)S(1)}, f32[432,128]{1,0:T(8,128)S(1)}, f32[432,128]{1,0:T(8,128)S(1)}, bf16[4,2,4,224,256]{4,3,2,1,0:T(8,128)(2,1)S(1)}) custom-call(f32[4,2,4,216,256]{4,3,2,1,0:T(8,128)} %bitcast.21, f32[432,128]{1,0:T(8,128)S(1)} %bitcast.18, f32[432,128]{1,0:T(8,128)S(1)} %bitcast.19, f32[432,128]{1,0:T(8,128)S(1)} %bitcast.20), custom_call_target="tpu_custom_call" | custom-call | tf_op jit(solution)/shard_map/pallas_call | solution.py:464
  88.5 2.1 %slice.3 = bf16[4,2,4,216,256]{4,3,2,1,0:T(8,128)(2,1)} slice(bf16[4,2,4,224,256]{4,3,2,1,0:T(8,128)(2,1)S(1)} %get-tuple-element.11), slice={[0:4], [0:2], [0:4], [0:216], [0:256]} | slice | bytes 7077888 | tf_op jit(solution)/shard_map/slice | solution.py:503
  90.6 0.7 copy.17
  91.3 0.7 copy.18
  92.0 0.7 copy.19
Async XLA Ops:
  2.9 2.0 %copy-start = (bf16[27,256,256]{2,1,0:T(8,128)(2,1)S(1)}, bf16[27,256,256]{2,1,0:T(8,128)(2,1)}, u32[]{:S(2)}) copy-start(bf16[27,256,256]{2,1,0:T(8,128)(2,1)} %weights.1) | copy-start | bytes 10616836
  4.9 0.9 %copy-start.1 = (bf16[1,2,16,16,256]{4,3,2,1,0:T(8,128)(2,1)S(1)}, bf16[1,2,16,16,256]{4,3,2,1,0:T(8,128)(2,1)}, u32[]{:S(2)}) copy-start(bf16[1,2,16,16,256]{4,3,2,1,0:T(8,128)(2,1)} %param.10) | copy-start | bytes 786436
  5.9 0.7 copy-start.5
  6.5 0.7 copy-start.6
  7.2 18.6 %copy-start.2 = (f32[55296]{0:T(1024)S(1)}, f32[55296]{0:T(1024)}, u32[]{:S(2)}) copy-start(f32[55296]{0:T(1024)} %param.17) | copy-start | bytes 663556
  7.2 18.6 %copy-start.3 = (f32[55296]{0:T(1024)S(1)}, f32[55296]{0:T(1024)}, u32[]{:S(2)}) copy-start(f32[55296]{0:T(1024)} %param.18) | copy-start | bytes 663556
  7.2 18.6 %copy-start.4 = (f32[55296]{0:T(1024)S(1)}, f32[55296]{0:T(1024)}, u32[]{:S(2)}) copy-start(f32[55296]{0:T(1024)} %param.19) | copy-start | bytes 663556

commit v3 on v2

--- a/solution.py
+++ b/solution.py
@@ -25,18 +25,34 @@
     return real, imag
 
 
-def grad_kernel(
+def widen(block, rows):
+    extra = rows - block.shape[0]
+    if extra:
+        block = jnp.concatenate([block, jnp.zeros((extra, block.shape[1]), block.dtype)], axis=0)
+    return block.astype(jnp.bfloat16)
+
+
+def step_kernel(
     sizes,
     scale,
     norm_scale,
     features,
-    weights,
+    weights_far,
     head,
     materials,
     ports,
     permittivity,
     port_source,
+    master,
+    moment,
+    second,
+    new_master,
+    new_moment,
+    new_second,
+    full,
     grad,
+    blocks,
+    weights,
     halo,
     near_taps,
     turned,
@@ -44,14 +60,51 @@
     d_pad,
     edge_out,
     edge_in,
+    pair_in,
+    group_out,
+    group_in,
+    line_out,
+    line_in,
+    narrow,
+    weight_sem,
     send,
     recv,
+    pair_send,
+    pair_recv,
+    group_send,
+    group_recv,
+    line_send,
+    line_recv,
+    line_back_send,
+    line_back_recv,
+    group_back_send,
+    group_back_recv,
+    pair_back_send,
+    pair_back_recv,
 ):
     line, grid_w = sizes
     depth, cells, channels = features.shape
+    groups, _, _, padded, width = full.shape
+    rows = grad.shape[0] // (groups * 2 * line)
     wide = 3 * channels
     dp = lax.axis_index("dp")
     here = lax.axis_index("slab")
+    mine = dp // 2
+    core = dp % 2
+    sibling = (mine * 2 + 1 - core, here)
+
+    def group_at(step):
+        return (mine + step + groups) % groups
+
+    def slab_at(step):
+        return (here + step + line) % line
+
+    def group_device(step):
+        return (group_at(step) * 2 + core, here)
+
+    def line_device(step):
+        return (dp, slab_at(step))
+
     has_low = here > 0
     has_high = here < line - 1
     low = (dp, here - 1)
@@ -90,16 +143,75 @@
         pl.when(has_low)(to_low.wait_send)
         pl.when(has_high)(to_high.wait_send)
 
+    def remote_pair(source, target, send_sem, recv_sem, device):
+        return pltpu.make_async_remote_copy(
+            src_ref=source,
+            dst_ref=target,
+            send_sem=send_sem,
+            recv_sem=recv_sem,
+            device_id=device,
+            device_id_type=pl.DeviceIdType.MESH,
+        )
+
+    def block_rows(group, side, slab):
+        first = ((group * 2 + side) * line + slab) * rows
+        return pl.ds(pl.multiple_of(first, 8), rows)
+
+    def block_at(group, side, slab):
+        if rows % 8:
+            return blocks.at[(group * 2 + side) * line + slab]
+        return grad.at[block_rows(group, side, slab)]
+
+    def pair_copy(group, slab):
+        return remote_pair(
+            block_at(group, 1 - core, slab),
+            pair_in.at[group, slab],
+            pair_send.at[group, slab],
+            pair_recv.at[group, slab],
+            sibling,
+        )
+
+    def pair_sum(group, slab):
+        pair_copy(group, slab).wait_recv()
+        return block_at(group, core, slab)[...] + pair_in[group, slab]
+
+    def group_copy(k, j):
+        return remote_pair(
+            group_out.at[k - 1, j],
+            group_in.at[k - 1, j],
+            group_send.at[k - 1, j],
+            group_recv.at[k - 1, j],
+            group_device(k),
+        )
+
+    def line_copy(j):
+        return remote_pair(
+            line_out.at[j - 1], line_in.at[j - 1], line_send.at[j - 1], line_recv.at[j - 1], line_device(j)
+        )
+
+    def line_back(j):
+        spot = full.at[mine, core, here]
+        return remote_pair(spot, spot, line_back_send.at[j - 1], line_back_recv.at[j - 1], line_device(j))
+
+    def group_back(k, j):
+        spot = full.at[mine, core, slab_at(-j)]
+        return remote_pair(
+            spot, spot, group_back_send.at[k - 1, j], group_back_recv.at[k - 1, j], group_device(k)
+        )
+
+    def pair_back(k, j):
+        spot = full.at[group_at(-k), core, slab_at(-j)]
+        return remote_pair(spot, spot, pair_back_send.at[k, j], pair_back_recv.at[k, j], sibling)
+
+    weight_copy = pltpu.make_async_copy(weights_far, weights, weight_sem)
+    weight_copy.start()
+    others = [sibling]
+    others += [group_device(k) for k in range(1, groups)]
+    others += [line_device(j) for j in range(1, line)]
     barrier = pltpu.get_barrier_semaphore()
-    for there, device in ((has_low, low), (has_high, high)):
-
-        @pl.when(there)
-        def _(device=device):
-            pl.semaphore_signal(
-                barrier, inc=1, device_id=device, device_id_type=pl.DeviceIdType.MESH
-            )
-
-    pl.semaphore_wait(barrier, jnp.where(has_low, 1, 0) + jnp.where(has_high, 1, 0))
+    for device in others:
+        pl.semaphore_signal(barrier, inc=1, device_id=device, device_id_type=pl.DeviceIdType.MESH)
+    pl.semaphore_wait(barrier, len(others))
 
     start(0)
     for side, there in ((0, has_low), (1, has_high)):
@@ -147,6 +259,7 @@
 
     for plane in range(depth):
         lay(plane + 1, features[plane])
+    weight_copy.wait()
     factor[...] = taps(1)
     finish(0)
     lay(0, halo[0])
@@ -222,179 +335,41 @@
         d_pre = d_hidden * factor[plane * cells : (plane + 1) * cells]
         d_pad[plane, grid_w : grid_w + cells] = d_pre.astype(jnp.bfloat16)
 
+    ready = 0
+    group_rows = 2 * line * rows
     for shift_z in range(3):
         left = turned[:, shift_z * cells : (shift_z + depth) * cells]
         for shift_y in range(3):
             top = (2 - shift_y) * grid_w
             first = 9 * shift_z + 3 * shift_y
-            grad[first : first + 3] = jnp.dot(
+            first = first * channels
+            grad[first : first + wide] = jnp.dot(
                 left,
                 d_pad[:, top : top + cells].reshape(depth * cells, channels),
                 preferred_element_type=jnp.float32,
-            ).reshape(3, channels, channels)
-
-
-def local_grad(features, weights, head_proj, materials, ports, permittivity, port_source, scale):
-    depth, grid_h, grid_w, channels = features.shape
-    cells = grid_h * grid_w
-    line = lax.axis_size("slab")
-    all_cells = depth * cells * lax.axis_size("dp") * line
-    norm_scale = float(np.float32(2.0) / np.sqrt(np.float32(all_cells)))
-    vmem = pl.BlockSpec(memory_space=pltpu.VMEM)
-    smem = pl.BlockSpec(memory_space=pltpu.SMEM)
-    tall = cells + 2 * grid_w
-    return pl.pallas_call(
-        functools.partial(grad_kernel, (line, grid_w), scale, norm_scale),
-        out_shape=jax.ShapeDtypeStruct((27, channels, channels), jnp.float32),
-        in_specs=[vmem] * 5 + [smem] * 2,
-        out_specs=vmem,
-        scratch_shapes=[
-            pltpu.VMEM((2, cells, channels), jnp.bfloat16),
-            pltpu.VMEM((depth + 2, tall, 3 * channels), jnp.bfloat16),
-            pltpu.VMEM((3 * channels, (depth + 2) * cells), jnp.bfloat16),
-            pltpu.VMEM((depth * cells, channels), jnp.float32),
-            pltpu.VMEM((depth, tall, channels), jnp.bfloat16),
-            pltpu.VMEM((2, 2, 8, cells), jnp.float32),
-            pltpu.VMEM((2, 2, 8, cells), jnp.float32),
-            pltpu.SemaphoreType.DMA((3, 2)),
-            pltpu.SemaphoreType.DMA((3, 2)),
-        ],
-        compiler_params=pltpu.CompilerParams(
-            collective_id=1, has_side_effects=True, vmem_limit_bytes=48 * 1024 * 1024
-        ),
-    )(
-        features.reshape(depth, cells, channels),
-        weights,
-        jnp.pad(head_proj.T, ((0, 14), (0, 0))),
-        materials.reshape(depth, cells),
-        ports.reshape(depth, cells),
-        permittivity,
-        port_source,
-    )
-
-
-def widen(block, rows):
-    extra = rows - block.shape[0]
-    if extra:
-        block = jnp.concatenate([block, jnp.zeros((extra, block.shape[1]), block.dtype)], axis=0)
-    return block.astype(jnp.bfloat16)
-
-
-def share_kernel(
-    scale,
-    grad,
-    master,
-    moment,
-    second,
-    new_master,
-    new_moment,
-    new_second,
-    full,
-    pair_in,
-    group_out,
-    group_in,
-    line_out,
-    line_in,
-    narrow,
-    pair_send,
-    pair_recv,
-    group_send,
-    group_recv,
-    line_send,
-    line_recv,
-    line_back_send,
-    line_back_recv,
-    group_back_send,
-    group_back_recv,
-    pair_back_send,
-    pair_back_recv,
-):
-    groups, _, line, rows, width = grad.shape
-    padded = full.shape[3]
-    dp = lax.axis_index("dp")
-    here = lax.axis_index("slab")
-    mine = dp // 2
-    core = dp % 2
-    sibling = (mine * 2 + 1 - core, here)
-
-    def group_at(step):
-        return (mine + step + groups) % groups
-
-    def slab_at(step):
-        return (here + step + line) % line
-
-    def group_device(step):
-        return (group_at(step) * 2 + core, here)
-
-    def line_device(step):
-        return (dp, slab_at(step))
-
-    def remote(source, target, send, recv, device):
-        return pltpu.make_async_remote_copy(
-            src_ref=source,
-            dst_ref=target,
-            send_sem=send,
-            recv_sem=recv,
-            device_id=device,
-            device_id_type=pl.DeviceIdType.MESH,
-        )
-
-    def pair_copy(k):
-        return remote(
-            grad.at[group_at(k), 1 - core], pair_in.at[k], pair_send.at[k], pair_recv.at[k], sibling
-        )
-
-    def group_copy(k, j):
-        return remote(
-            group_out.at[k - 1, j],
-            group_in.at[k - 1, j],
-            group_send.at[k - 1, j],
-            group_recv.at[k - 1, j],
-            group_device(k),
-        )
-
-    def line_copy(j):
-        return remote(
-            line_out.at[j - 1], line_in.at[j - 1], line_send.at[j - 1], line_recv.at[j - 1], line_device(j)
-        )
-
-    def line_back(j):
-        spot = full.at[mine, core, here]
-        return remote(spot, spot, line_back_send.at[j - 1], line_back_recv.at[j - 1], line_device(j))
-
-    def group_back(k, j):
-        spot = full.at[mine, core, slab_at(-j)]
-        return remote(
-            spot, spot, group_back_send.at[k - 1, j], group_back_recv.at[k - 1, j], group_device(k)
-        )
-
-    def pair_back(k, j):
-        spot = full.at[group_at(-k), core, slab_at(-j)]
-        return remote(spot, spot, pair_back_send.at[k, j], pair_back_recv.at[k, j], sibling)
-
-    others = [sibling]
-    others += [group_device(k) for k in range(1, groups)]
-    others += [line_device(j) for j in range(1, line)]
-    barrier = pltpu.get_barrier_semaphore()
-    for device in others:
-        pl.semaphore_signal(barrier, inc=1, device_id=device, device_id_type=pl.DeviceIdType.MESH)
-    pl.semaphore_wait(barrier, len(others))
+            )
+            while rows % 8 == 0 and ready < groups and (ready + 1) * group_rows <= first + wide:
+                for slab in range(line):
+                    pair_copy(ready, slab).start()
+                ready += 1
+    if rows % 8:
+        for spot in range(groups * 2 * line):
+            blocks[spot] = grad[spot * rows : (spot + 1) * rows]
+        for group in range(groups):
+            for slab in range(line):
+                pair_copy(group, slab).start()
 
     group_order = list(range(1, groups)) + [0]
     line_order = list(range(1, line)) + [0]
-    for k in group_order:
-        pair_copy(k).start()
     for k in group_order[:-1]:
-        pair_copy(k).wait_recv()
         for j in line_order:
             slab = slab_at(j)
-            group_out[k - 1, j] = widen(grad[group_at(k), core, slab] + pair_in[k, slab], padded)
+            group_out[k - 1, j] = widen(pair_sum(group_at(k), slab), padded)
             group_copy(k, j).start()
-    pair_copy(0).wait_recv()
     total = None
     for j in line_order:
         slab = slab_at(j)
-        total = grad[mine, core, slab] + pair_in[0, slab]
+        total = pair_sum(mine, slab)
         for k in range(1, groups):
             group_copy(k, j).wait_recv()
             total = total + group_in[k - 1, j].astype(jnp.float32)[:rows]
@@ -440,8 +415,8 @@
         for k in range(groups):
             pair_back(k, j).wait_recv()
     for k in range(groups):
-        pair_copy(k).wait_send()
         for j in range(line):
+            pair_copy(k, j).wait_send()
             pair_back(k, j).wait_send()
             if k:
                 group_copy(k, j).wait_send()
@@ -451,35 +426,56 @@
         line_back(j).wait_send()
 
 
-def share_and_step(grad, master, moment, second, scale):
-    rows_all, width = grad.shape
+def whole_step(features, weights, head_proj, codes, tables, states):
+    depth, grid_h, grid_w, channels = features.shape
+    cells = grid_h * grid_w
+    line = lax.axis_size("slab")
     groups = lax.axis_size("dp") // 2
-    line = lax.axis_size("slab")
+    all_cells = depth * cells * groups * 2 * line
+    scale = float(np.float32(1.0) / np.sqrt(np.float32(27 * channels)))
+    norm_scale = float(np.float32(2.0) / np.sqrt(np.float32(all_cells)))
+    rows_all = 27 * channels
     rows = rows_all // (groups * 2 * line)
     padded = -(-rows // 16) * 16
-    flat = (master.size // 128, 128)
+    flat = (rows * channels // 128, 128)
+    tall = cells + 2 * grid_w
+    spare = (groups * 2 * line, rows, channels) if rows % 8 else (1, 8, 128)
     vmem = pl.BlockSpec(memory_space=pltpu.VMEM)
+    smem = pl.BlockSpec(memory_space=pltpu.SMEM)
     dma = pltpu.SemaphoreType.DMA
     state = jax.ShapeDtypeStruct(flat, jnp.float32)
     out = pl.pallas_call(
-        functools.partial(share_kernel, scale),
+        functools.partial(step_kernel, (line, grid_w), scale, norm_scale),
         out_shape=[
             state,
             state,
             state,
-            jax.ShapeDtypeStruct((groups, 2, line, padded, width), jnp.bfloat16),
+            jax.ShapeDtypeStruct((groups, 2, line, padded, channels), jnp.bfloat16),
         ],
-        in_specs=[vmem] * 4,
+        in_specs=[vmem, pl.BlockSpec(memory_space=pl.ANY)] + [vmem] * 3 + [smem] * 2 + [vmem] * 3,
         out_specs=[vmem] * 4,
         scratch_shapes=[
-            pltpu.VMEM((groups, line, rows, width), jnp.float32),
-            pltpu.VMEM((groups - 1, line, padded, width), jnp.bfloat16),
-            pltpu.VMEM((groups - 1, line, padded, width), jnp.bfloat16),
-            pltpu.VMEM((line - 1, padded, width), jnp.bfloat16),
-            pltpu.VMEM((line - 1, padded, width), jnp.bfloat16),
+            pltpu.VMEM((rows_all, channels), jnp.float32),
+            pltpu.VMEM(spare, jnp.float32),
+            pltpu.VMEM((27, channels, channels), jnp.bfloat16),
+            pltpu.VMEM((2, cells, channels), jnp.bfloat16),
+            pltpu.VMEM((depth + 2, tall, 3 * channels), jnp.bfloat16),
+            pltpu.VMEM((3 * channels, (depth + 2) * cells), jnp.bfloat16),
+            pltpu.VMEM((depth * cells, channels), jnp.float32),
+            pltpu.VMEM((depth, tall, channels), jnp.bfloat16),
+            pltpu.VMEM((2, 2, 8, cells), jnp.float32),
+            pltpu.VMEM((2, 2, 8, cells), jnp.float32),
+            pltpu.VMEM((groups, line, rows, channels), jnp.float32),
+            pltpu.VMEM((groups - 1, line, padded, channels), jnp.bfloat16),
+            pltpu.VMEM((groups - 1, line, padded, channels), jnp.bfloat16),
+            pltpu.VMEM((line - 1, padded, channels), jnp.bfloat16),
+            pltpu.VMEM((line - 1, padded, channels), jnp.bfloat16),
             pltpu.VMEM(flat, jnp.float32),
-            dma((groups,)),
-            dma((groups,)),
+            dma,
+            dma((3, 2)),
+            dma((3, 2)),
+            dma((groups, line)),
+            dma((groups, line)),
             dma((groups - 1, line)),
             dma((groups - 1, line)),
             dma((line - 1,)),
@@ -492,16 +488,18 @@
             dma((groups, line)),
         ],
         compiler_params=pltpu.CompilerParams(
-            collective_id=0, has_side_effects=True, vmem_limit_bytes=48 * 1024 * 1024
+            collective_id=0, has_side_effects=True, vmem_limit_bytes=58 * 1024 * 1024
         ),
     )(
-        grad.reshape(groups, 2, line, rows, width),
-        master.reshape(flat),
-        moment.reshape(flat),
-        second.reshape(flat),
+        features.reshape(depth, cells, channels),
+        weights,
+        jnp.pad(head_proj.T, ((0, 14), (0, 0))),
+        *[part.reshape(depth, cells) for part in codes],
+        *tables,
+        *[part.reshape(flat) for part in states],
     )
-    full = out[3][:, :, :, :rows].reshape(rows_all, width)
-    return [part.reshape(-1) for part in out[:3]] + [full]
+    full = out[3][:, :, :, :rows].reshape(weights.shape)
+    return tuple(part.reshape(-1) for part in out[:3]) + (full,)
 
 
 def body(
@@ -516,21 +514,14 @@
     moment,
     second,
 ):
-    channels = features.shape[-1]
-    scale = float(np.float32(1.0) / np.sqrt(np.float32(27 * channels)))
-    grad = local_grad(
+    return whole_step(
         features[0],
         kernel,
         head_proj,
-        material_ids[0],
-        port_ids[0],
-        permittivity,
-        port_source,
-        scale,
-    ).reshape(27 * channels, channels)
-    new_master, new_moment, new_second, full = share_and_step(grad, master, moment, second, scale)
-    new_kernel = full.reshape(kernel.shape)
-    return (new_master, new_moment, new_second, new_kernel)
+        (material_ids[0], port_ids[0]),
+        (permittivity, port_source),
+        (master, moment, second),
+    )
 
 
 def solution(mesh):

time: 93.6 us -> 90.1 us (0.963)
  Pallas kernels: 81.2 us -> 77.7 us
    unnamed x17 -> x9, local copies, waits for them, and re-layouts: 6.42 us -> 2.11 us
    pallas_call x2 -> x1, Pallas kernels: 81.2 us -> 77.7 us  [whole_step(): pl.pallas_call(functools.partial(step_kernel, (line, grid_w), scale, norm...]
    slice x1, local copies, waits for them, and re-layouts: 2.08 us -> 4.09 us  [whole_step(): full = out[3][:, :, :, :rows].reshape(weights.shape)]
    another operation x2, local copies, waits for them, and re-layouts: 1.6 us -> 2.76 us  [whole_step(): part.reshape(depth, cells)]
where the time goes in v3:
time: 90.1 us; the launch traced here: 88.6 us
  Pallas kernels  77.7 us (86%)
  local copies, waits for them, and re-layouts  10.2 us (11%)
    pallas_call x1, Pallas kernels, whole_step(): pl.pallas_call(functools.partial(step_kernel, (line, grid_w), scale, norm...  77.7 us
    slice x1, local copies, waits for them, and re-layouts, whole_step(): full = out[3][:, :, :, :rows].reshape(weights.shape)  4.09 us
    another operation x2, local copies, waits for them, and re-layouts, whole_step(): part.reshape(depth, cells)  2.76 us
    unnamed x9, local copies, waits for them, and re-layouts  2.11 us

profile of v3, /device:TPU:21, one launch (start us, length us, event | category | flops | bytes accessed | tf_op | source)
XLA Modules:
  0.0 88.6 jit_solution(10031515279161746668)
XLA Ops:
  0.6 1.4 %reshape_squeeze.10.materials = s32[2,256]{1,0:T(2,128)} reshape(s32[1,2,16,16]{3,2,1,0:T(8,128)} %param.13) | data formatting | bytes 4096 | tf_op jit(solution)/shard_map/reshape;squeeze | solution.py:497
  2.0 1.4 %reshape_squeeze.11.ports = s32[2,256]{1,0:T(2,128)} reshape(s32[1,2,16,16]{3,2,1,0:T(8,128)} %param.14) | data formatting | bytes 4096 | tf_op jit(solution)/shard_map/reshape;squeeze | solution.py:497
  3.4 1.3 %pad.4.head = bf16[16,256]{1,0:T(8,128)(2,1)} pad(bf16[2,256]{1,0:T(2,128)(2,1)} %bitcast.21, bf16[]{:T(256)} %constant.2.clone.1), padding=0_14x0_0 | pad | bytes 9218 | tf_op jit(solution)/shard_map/jit(_pad)/pad | solution.py:496
  4.7 77.7 %shard_map.129 = (f32[432,128]{1,0:T(8,128)}, f32[432,128]{1,0:T(8,128)}, f32[432,128]{1,0:T(8,128)}, bf16[4,2,4,224,256]{4,3,2,1,0:T(8,128)(2,1)}) custom-call(bf16[2,256,256]{2,1,0:T(8,128)(2,1)} %bitcast.14, bf16[27,256,256]{2,1,0:T(8,128)(2,1)} %weights_far.1, bf16[16,256]{1,0:T(8,128)(2,1)} %pad.4.head, s32[2,256]{1,0:T(2,128)} %reshape_squeeze.10.materials, ...), custom_call_target="tpu_custom_call" | custom-call | tf_op jit(solution)/shard_map/pallas_call | solution.py:447
  82.4 0.0 copy-start.2
  82.4 0.0 copy-start.1
  82.4 0.0 copy-start
  82.4 4.1 %slice.3 = bf16[4,2,4,216,256]{4,3,2,1,0:T(8,128)(2,1)} slice(bf16[4,2,4,224,256]{4,3,2,1,0:T(8,128)(2,1)} %get-tuple-element.11), slice={[0:4], [0:2], [0:4], [0:216], [0:256]} | slice | bytes 7077888 | tf_op jit(solution)/shard_map/slice | solution.py:501
  86.5 0.0 copy-done.2
  86.5 0.7 copy.17
  87.2 0.0 copy-done.1
  87.2 0.7 copy.18
  87.9 0.0 copy-done
  87.9 0.7 copy.19
Async XLA Ops:
  82.4 4.1 %copy-start.2 = (f32[432,128]{1,0:T(8,128)S(1)}, f32[432,128]{1,0:T(8,128)}, u32[]{:S(2)}) copy-start(f32[432,128]{1,0:T(8,128)} %get-tuple-element.8) | copy-start | bytes 663556
  82.4 4.8 %copy-start.1 = (f32[432,128]{1,0:T(8,128)S(1)}, f32[432,128]{1,0:T(8,128)}, u32[]{:S(2)}) copy-start(f32[432,128]{1,0:T(8,128)} %get-tuple-element.9) | copy-start | bytes 663556
  82.4 5.5 %copy-start = (f32[432,128]{1,0:T(8,128)S(1)}, f32[432,128]{1,0:T(8,128)}, u32[]{:S(2)}) copy-start(f32[432,128]{1,0:T(8,128)} %get-tuple-element.10) | copy-start | bytes 663556

commit v4 on v3

--- a/solution.py
+++ b/solution.py
@@ -37,7 +37,7 @@
     scale,
     norm_scale,
     features,
-    weights_far,
+    weights,
     head,
     materials,
     ports,
@@ -52,7 +52,6 @@
     full,
     grad,
     blocks,
-    weights,
     halo,
     near_taps,
     turned,
@@ -66,7 +65,6 @@
     line_out,
     line_in,
     narrow,
-    weight_sem,
     send,
     recv,
     pair_send,
@@ -203,8 +201,6 @@
         spot = full.at[group_at(-k), core, slab_at(-j)]
         return remote_pair(spot, spot, pair_back_send.at[k, j], pair_back_recv.at[k, j], sibling)
 
-    weight_copy = pltpu.make_async_copy(weights_far, weights, weight_sem)
-    weight_copy.start()
     others = [sibling]
     others += [group_device(k) for k in range(1, groups)]
     others += [line_device(j) for j in range(1, line)]
@@ -259,7 +255,6 @@
 
     for plane in range(depth):
         lay(plane + 1, features[plane])
-    weight_copy.wait()
     factor[...] = taps(1)
     finish(0)
     lay(0, halo[0])
@@ -452,12 +447,11 @@
             state,
             jax.ShapeDtypeStruct((groups, 2, line, padded, channels), jnp.bfloat16),
         ],
-        in_specs=[vmem, pl.BlockSpec(memory_space=pl.ANY)] + [vmem] * 3 + [smem] * 2 + [vmem] * 3,
+        in_specs=[vmem] * 5 + [smem] * 2 + [vmem] * 3,
         out_specs=[vmem] * 4,
         scratch_shapes=[
             pltpu.VMEM((rows_all, channels), jnp.float32),
             pltpu.VMEM(spare, jnp.float32),
-            pltpu.VMEM((27, channels, channels), jnp.bfloat16),
             pltpu.VMEM((2, cells, channels), jnp.bfloat16),
             pltpu.VMEM((depth + 2, tall, 3 * channels), jnp.bfloat16),
             pltpu.VMEM((3 * channels, (depth + 2) * cells), jnp.bfloat16),
@@ -471,7 +465,6 @@
             pltpu.VMEM((line - 1, padded, channels), jnp.bfloat16),
             pltpu.VMEM((line - 1, padded, channels), jnp.bfloat16),
             pltpu.VMEM(flat, jnp.float32),
-            dma,
             dma((3, 2)),
             dma((3, 2)),
             dma((groups, line)),
@@ -488,7 +481,7 @@
             dma((groups, line)),
         ],
         compiler_params=pltpu.CompilerParams(
-            collective_id=0, has_side_effects=True, vmem_limit_bytes=58 * 1024 * 1024
+            collective_id=0, has_side_effects=True, vmem_limit_bytes=36 * 1024 * 1024
         ),
     )(
         features.reshape(depth, cells, channels),

time: 90.1 us -> 90.8 us (level)
  local copies, waits for them, and re-layouts: 10.2 us -> 13.6 us
  Pallas kernels: 77.7 us -> 75 us
    unnamed x9 -> x17, local copies, waits for them, and re-layouts: 2.11 us -> 9.21 us
    pallas_call x1, Pallas kernels: 77.7 us -> 75 us  [whole_step(): pl.pallas_call(functools.partial(step_kernel, (line, grid_w), scale, norm...]
    slice x1, local copies, waits for them, and re-layouts: 4.09 us -> 2.08 us  [whole_step(): full = out[3][:, :, :, :rows].reshape(weights.shape)]
    another operation x2, local copies, waits for them, and re-layouts: 2.76 us -> 1.6 us  [whole_step(): part.reshape(depth, cells)]
where the time goes in v4:
time: 90.8 us; the launch traced here: 89.2 us
  Pallas kernels  75 us (83%)
  local copies, waits for them, and re-layouts  13.6 us (15%)
    pallas_call x1, Pallas kernels, whole_step(): pl.pallas_call(functools.partial(step_kernel, (line, grid_w), scale, norm...  75 us
    unnamed x17, local copies, waits for them, and re-layouts  9.21 us
    slice x1, local copies, waits for them, and re-layouts, whole_step(): full = out[3][:, :, :, :rows].reshape(weights.shape)  2.08 us

profile of v4, /device:TPU:21, one launch (start us, length us, event | category | flops | bytes accessed | tf_op | source)
XLA Modules:
  0.0 89.2 jit_solution(7183200277805988417)
XLA Ops:
  0.6 0.8 reshape_squeeze.10.materials
  1.4 0.8 reshape_squeeze.11.ports
  2.2 0.7 pad.4.head
  2.9 0.0 copy-start
  2.9 2.0 %copy-done = bf16[27,256,256]{2,1,0:T(8,128)(2,1)S(1)} copy-done((bf16[27,256,256]{2,1,0:T(8,128)(2,1)S(1)}, bf16[27,256,256]{2,1,0:T(8,128)(2,1)}, u32[]{:S(2)}) %copy-start) | copy-done | bytes 3538968
  4.9 0.0 copy-start.1
  4.9 0.9 %copy-done.1 = bf16[1,2,16,16,256]{4,3,2,1,0:T(8,128)(2,1)S(1)} copy-done((bf16[1,2,16,16,256]{4,3,2,1,0:T(8,128)(2,1)S(1)}, bf16[1,2,16,16,256]{4,3,2,1,0:T(8,128)(2,1)}, u32[]{:S(2)}) %copy-start.1) | copy-done | bytes 262168
  5.9 0.0 copy-start.2
  5.9 0.9 %copy-done.2 = f32[55296]{0:T(1024)S(1)} copy-done((f32[55296]{0:T(1024)S(1)}, f32[55296]{0:T(1024)}, u32[]{:S(2)}) %copy-start.2) | copy-done | bytes 221208
  6.8 0.0 copy-start.3
  6.8 0.9 %copy-done.3 = f32[55296]{0:T(1024)S(1)} copy-done((f32[55296]{0:T(1024)S(1)}, f32[55296]{0:T(1024)}, u32[]{:S(2)}) %copy-start.3) | copy-done | bytes 221208
  7.7 0.0 copy-start.4
  7.7 0.9 %copy-done.4 = f32[55296]{0:T(1024)S(1)} copy-done((f32[55296]{0:T(1024)S(1)}, f32[55296]{0:T(1024)}, u32[]{:S(2)}) %copy-start.4) | copy-done | bytes 221208
  8.7 0.0 copy-start.5
  8.7 0.7 copy-done.5
  9.4 0.0 copy-start.6
  9.4 0.7 copy-done.6
  10.0 75.0 %shard_map.129 = (f32[432,128]{1,0:T(8,128)S(1)}, f32[432,128]{1,0:T(8,128)S(1)}, f32[432,128]{1,0:T(8,128)S(1)}, bf16[4,2,4,224,256]{4,3,2,1,0:T(8,128)(2,1)S(1)}) custom-call(bf16[2,256,256]{2,1,0:T(8,128)(2,1)S(1)} %bitcast.13, bf16[27,256,256]{2,1,0:T(8,128)(2,1)S(1)} %copy-done, bf16[16,256]{1,0:T(8,128)(2,1)S(1)} %pad.4.head, ...), custom_call_target="tpu_custom_call" | custom-call | tf_op jit(solution)/shard_map/pallas_call | solution.py:442
  85.0 2.1 %slice.3 = bf16[4,2,4,216,256]{4,3,2,1,0:T(8,128)(2,1)} slice(bf16[4,2,4,224,256]{4,3,2,1,0:T(8,128)(2,1)S(1)} %get-tuple-element.11), slice={[0:4], [0:2], [0:4], [0:216], [0:256]} | slice | bytes 7077888 | tf_op jit(solution)/shard_map/slice | solution.py:494
  87.1 0.7 copy.17
  87.8 0.7 copy.18
  88.5 0.7 copy.19
Async XLA Ops:
  2.9 2.0 %copy-start = (bf16[27,256,256]{2,1,0:T(8,128)(2,1)S(1)}, bf16[27,256,256]{2,1,0:T(8,128)(2,1)}, u32[]{:S(2)}) copy-start(bf16[27,256,256]{2,1,0:T(8,128)(2,1)} %weights.1) | copy-start | bytes 10616836
  4.9 0.9 %copy-start.1 = (bf16[1,2,16,16,256]{4,3,2,1,0:T(8,128)(2,1)S(1)}, bf16[1,2,16,16,256]{4,3,2,1,0:T(8,128)(2,1)}, u32[]{:S(2)}) copy-start(bf16[1,2,16,16,256]{4,3,2,1,0:T(8,128)(2,1)} %param.10) | copy-start | bytes 786436
  5.9 0.9 %copy-start.2 = (f32[55296]{0:T(1024)S(1)}, f32[55296]{0:T(1024)}, u32[]{:S(2)}) copy-start(f32[55296]{0:T(1024)} %param.17) | copy-start | bytes 663556
  6.8 0.9 %copy-start.3 = (f32[55296]{0:T(1024)S(1)}, f32[55296]{0:T(1024)}, u32[]{:S(2)}) copy-start(f32[55296]{0:T(1024)} %param.18) | copy-start | bytes 663556
  7.7 0.9 %copy-start.4 = (f32[55296]{0:T(1024)S(1)}, f32[55296]{0:T(1024)}, u32[]{:S(2)}) copy-start(f32[55296]{0:T(1024)} %param.19) | copy-start | bytes 663556
  8.7 0.7 copy-start.5
  9.4 0.7 copy-start.6
